TPU v7x, 768 devices: a whole 4x8x12 slice. The times are simulated.
768 devices in a mesh: section: 12 (over z), mp: 8 (over y_hi, core), dp: 8 (over x, y_lo).
Axes of the slice: x: 4, y: 8 (y_hi: 4, y_lo: 2; y = y_hi * 2 + y_lo), z: 12, core: 2. Of those that a mesh axis runs over, the one named last changes fastest.
Arguments:
- context: bfloat16 [12, 1024, 6144], P('section', None, 'mp'), may hold values from -6 to 6
- out_weight: bfloat16 [12, 6144, 8, 8, 192], P('section', 'mp', None, 'dp'), may hold values from -0.078125 to 0.078125
- residual: bfloat16 [12, 1024, 12288], P('section', None, ('mp', 'dp')), may hold values from -6 to 6
- layer_norm_gain: float32 [12, 12288], P('section', 'mp'), may hold values from 0.25 to 1.75
- layer_norm_bias: float32 [12, 12288], P('section', 'mp'), may hold values from -3 to 3
- ln_cotangent: bfloat16 [12, 1024, 12288], P('section', 'dp', 'mp'), may hold values from -6 to 6
Outputs:
- layer_norm_output: bfloat16 [12, 1024, 12288], P('section', 'dp', 'mp')
- resid_grad: bfloat16 [12, 1024, 12288], P('section', 'dp', 'mp')
All inputs are finite; a program needn't handle non-finite values.
Results may differ from a plain program's by a relative error of at most 0.0047.
Values may be sent and summed in bfloat16 or wider, within the bound.
No kernel may reach another device: no remote copies, remote signals or barrier semaphores. Data moves between devices by JAX's collectives and lax.ppermute only.
A program may use at most 64 MiB of HBM per device.

v0:
```python
import jax
import jax.numpy as jnp
from jax import lax
from jax.sharding import PartitionSpec as P

D = 12288


epsilon = 1e-05


def passed_along(x, axis, by):
    devices = lax.axis_size(axis)
    return lax.ppermute(x, axis, [(i, (i + by) % devices) for i in range(devices)])


def from_everyone(x, axis):
    copies = jnp.broadcast_to(x, (lax.axis_size(axis), *x.shape))
    return lax.all_to_all(copies, axis, split_axis=0, concat_axis=0, tiled=True)


def over_copies(x, axis):
    everything = from_everyone(x, axis)
    return jnp.sum(everything, axis=0)


def together(arrays, axis):
    ends = [0]
    for a in arrays:
        ends.append(ends[-1] + a.size)
    total = over_copies(jnp.concatenate([a.ravel() for a in arrays]), axis)
    return tuple((total[b:e].reshape(a.shape) for a, b, e in zip(arrays, ends, ends[1:])))


def cross_section(values):
    return passed_along(values, "section", 1)


def relayout(values):
    return lax.all_to_all(values, "dp", split_axis=0, concat_axis=1, tiled=True)


def local(context, out_weight, residual, layer_norm_gain, layer_norm_bias, ln_cotangent):
    local_ctx = context[0]
    weights = out_weight[0]
    weights = weights.reshape(weights.shape[0], weights.shape[1], weights.shape[3])
    summed = lax.psum_scatter(
        jnp.einsum("th,hjr->jtr", local_ctx, weights, preferred_element_type=jnp.float32),
        "mp",
        scatter_dimension=0,
        tiled=True,
    )
    section_out = (residual[0].astype(jnp.float32) + summed[0]).astype(jnp.bfloat16)
    arrived = relayout(cross_section(section_out))
    arrived = arrived.astype(jnp.float32)
    norm_gain_row = layer_norm_gain[0][None, :]
    gain_scaled = ln_cotangent[0].astype(jnp.float32) * norm_gain_row
    width = float(D)
    sum_one, sum_two, sum_three, sum_four = together(
        (
            jnp.sum(arrived, axis=-1, keepdims=True),
            jnp.sum(arrived * arrived, axis=-1, keepdims=True),
            jnp.sum(gain_scaled, axis=-1, keepdims=True),
            jnp.sum(gain_scaled * arrived, axis=-1, keepdims=True),
        ),
        "mp",
    )
    average = sum_one / width
    variance = sum_two / width - average * average
    inverse_deviation = lax.rsqrt(variance + epsilon)
    normalized_input = (arrived - average) * inverse_deviation
    input_mean = sum_three / width
    squared_mean = inverse_deviation * (sum_four / width - average * input_mean)
    layer_norm_output = (normalized_input * norm_gain_row + layer_norm_bias[0][None, :]).astype(
        jnp.bfloat16
    )
    incoming_gradient = (
        inverse_deviation * (gain_scaled - input_mean - normalized_input * squared_mean)
    ).astype(jnp.bfloat16)
    returned = passed_along(incoming_gradient, "section", -1)
    return (layer_norm_output[None], returned[None])


def solution(mesh):
    in_specs = (
        P("section", None, "mp"),
        P("section", "mp", None, "dp", None),
        P("section", None, ("mp", "dp")),
        P("section", "mp"),
        P("section", "mp"),
        P("section", "dp", "mp"),
    )
    out_specs = (P("section", "dp", "mp"), P("section", "dp", "mp"))
    return jax.shard_map(local, mesh=mesh, in_specs=in_specs, out_specs=out_specs, check_vma=False)
```

profile of v0, /device:TPU:1, one launch (start us, length us, event | category | flops | bytes accessed | tf_op | source)
XLA Modules:
  0.0 168.0 jit_solution(4978026600336690999)
XLA Ops:
  7.2 0.0 copy-start
  7.2 0.0 reduce-scatter.2.cloned.1.call-start
  7.2 1.6 copy-done
  8.8 5.9 %convolution_bitcast_fusion = f32[8,1024,192]{1,2,0:T(8,128)} fusion(bf16[1,768,8,1,192]{1,4,3,2,0:T(8,128)(2,1)S(1)} %copy-done, bf16[1,1024,768]{2,1,0:T(8,128)(2,1)} %param.6), kind=kOutput, calls=%fused_computation | convolution fusion | flops 2415919104 | bytes 10223616 | tf_op jit(solution)/shard_map/th,hjr->jtr/dot_general | solution.py:48
  14.7 0.0 copy-start.2
  14.7 0.0 reduce-scatter.2.cloned.1.call-update
  14.7 0.0 copy-start.1
  14.7 0.0 copy-start.3
  14.8 90.7 %reduce-scatter.2.cloned.1.call-done = f32[1,1024,192]{1,2,0:T(8,128)} async-done(((f32[8,1024,192]{1,2,0:T(8,128)}), f32[1,1024,192]{1,2,0:T(8,128)}) %reduce-scatter.2.cloned.1.call-update) | async-done | bytes 786448 | tf_op jit(solution)/shard_map/reduce_scatter | solution.py:47
  105.4 0.0 copy-done.2
  105.4 1.2 fusion.16
  106.6 1.9 %collective-permute-start = (bf16[1024,192]{0,1:T(8,128)(2,1)S(1)}, bf16[1024,192]{0,1:T(8,128)(2,1)S(1)}, u32[]{:S(2)}, u32[]{:S(2)}) collective-permute-start(bf16[1024,192]{0,1:T(8,128)(2,1)S(1)} %fusion.16), channel_id=1, source_target_pairs={{0,64},{64,128},{128,192},{192,256},{256,320},{320,384},{384,448},... | collective-permute-start | bytes 1179656 | tf_op jit(solution)/shard_map/ppermute | solution.py:14
  108.6 11.8 %collective-permute-done = bf16[1024,192]{0,1:T(8,128)(2,1)S(1)} collective-permute-done((bf16[1024,192]{0,1:T(8,128)(2,1)S(1)}, bf16[1024,192]{0,1:T(8,128)(2,1)S(1)}, u32[]{:S(2)}, u32[]{:S(2)}) %collective-permute-start) | collective-permute-done | bytes 393248 | tf_op jit(solution)/shard_map/ppermute | solution.py:14
  120.4 0.8 copy_bitcast_fusion
  121.2 3.5 %all-to-all-start = ((bf16[8,128,192]{1,2,0:T(8,128)(2,1)}), bf16[8,128,192]{1,2,0:T(8,128)(2,1)S(1)}, u32[]{:S(2)}, u32[]{:S(2)}) async-start(bf16[8,128,192]{1,2,0:T(8,128)(2,1)} %copy_bitcast_fusion), calls=%async_computation.1 | async-start | bytes 786432 | tf_op jit(solution)/shard_map/all_to_all | solution.py:40
  124.7 0.0 copy-done.1
  124.7 0.2 copy.19
  124.9 0.0 copy-done.3
  125.0 7.3 %all-to-all-done = bf16[8,128,192]{1,2,0:T(8,128)(2,1)S(1)} async-done(((bf16[8,128,192]{1,2,0:T(8,128)(2,1)}), bf16[8,128,192]{1,2,0:T(8,128)(2,1)S(1)}, u32[]{:S(2)}, u32[]{:S(2)}) %all-to-all-start) | async-done | bytes 393248 | tf_op jit(solution)/shard_map/all_to_all | solution.py:40
  132.3 0.2 convert_reduce_fusion
  132.5 0.3 fusion.4
  132.8 0.6 broadcast_in_dim.7
  133.4 7.5 %all-to-all-start.1 = ((f32[8,1,512]{2,1,0:T(1,128)}), f32[8,1,512]{2,1,0:T(1,128)S(1)}, u32[]{:S(2)}, u32[]{:S(2)}) async-start(f32[8,1,512]{2,1,0:T(1,128)} %broadcast_in_dim.7), calls=%async_computation.2 | async-start | bytes 32768 | tf_op jit(solution)/shard_map/all_to_all | solution.py:19
  140.9 0.7 reduce.6
  141.6 0.9 convert_element_type.72
  142.6 5.4 %all-to-all-done.1 = f32[8,1,512]{2,1,0:T(1,128)S(1)} async-done(((f32[8,1,512]{2,1,0:T(1,128)}), f32[8,1,512]{2,1,0:T(1,128)S(1)}, u32[]{:S(2)}, u32[]{:S(2)}) %all-to-all-start.1) | async-done | bytes 16416 | tf_op jit(solution)/shard_map/all_to_all | solution.py:19
  148.0 0.3 fusion.8
  148.4 3.3 %collective-permute-start.1 = (bf16[128,1536]{0,1:T(8,128)(2,1)S(1)}, bf16[128,1536]{0,1:T(8,128)(2,1)S(1)}, u32[]{:S(2)}, u32[]{:S(2)}) collective-permute-start(bf16[128,1536]{0,1:T(8,128)(2,1)S(1)} %fusion.8), channel_id=1, source_target_pairs={{0,704},{64,0},{128,64},{192,128},{256,192},{320,256},{384,320},{4... | collective-permute-start | bytes 1179656 | tf_op jit(solution)/shard_map/ppermute | solution.py:14
  151.7 1.6 fusion.12
  153.3 0.9 copy.21
  154.3 5.9 %collective-permute-done.1 = bf16[128,1536]{0,1:T(8,128)(2,1)S(1)} collective-permute-done((bf16[128,1536]{0,1:T(8,128)(2,1)S(1)}, bf16[128,1536]{0,1:T(8,128)(2,1)S(1)}, u32[]{:S(2)}, u32[]{:S(2)}) %collective-permute-start.1) | collective-permute-done | bytes 393248 | tf_op jit(solution)/shard_map/ppermute | solution.py:14
  160.2 0.9 copy.22
  (4 shorter events, 0.1 us)
Async XLA Ops:
  7.2 1.7 copy-start
  7.2 98.2 %reduce-scatter.2.cloned.1.call-start = ((), (), s32[]{:S(2)}) async-start(), calls=%async_computation.3 | async-start | bytes 7077888 | tf_op jit(solution)/shard_map/reduce_scatter | solution.py:47
  14.7 90.7 %copy-start.2 = (bf16[1,1024,192]{1,2,0:T(8,128)(2,1)S(1)}, bf16[1,1024,192]{1,2,0:T(8,128)(2,1)}, u32[]{:S(2)}) copy-start(bf16[1,1024,192]{1,2,0:T(8,128)(2,1)} %param.8) | copy-start | bytes 1179652
  14.7 110.0 %copy-start.1 = (bf16[1,128,1536]{2,1,0:T(8,128)(2,1)S(1)}, bf16[1,128,1536]{2,1,0:T(8,128)(2,1)}, u32[]{:S(2)}) copy-start(bf16[1,128,1536]{2,1,0:T(8,128)(2,1)} %param.11) | copy-start | bytes 1179652
  14.7 110.2 %copy-start.3 = (f32[1,1536]{1,0:T(1,128)S(1)}, f32[1,1536]{1,0:T(1,128)}, u32[]{:S(2)}) copy-start(f32[1,1536]{1,0:T(1,128)} %param.9) | copy-start | bytes 18436
  106.6 13.8 %collective-permute-start = (bf16[1024,192]{0,1:T(8,128)(2,1)S(1)}, bf16[1024,192]{0,1:T(8,128)(2,1)S(1)}, u32[]{:S(2)}, u32[]{:S(2)}) collective-permute-start(bf16[1024,192]{0,1:T(8,128)(2,1)S(1)} %fusion.16), channel_id=1, source_target_pairs={{0,64},{64,128},{128,192},{192,256},{256,320},{320,384},{384,448},... | collective-permute-start | bytes 1179656 | tf_op jit(solution)/shard_map/ppermute | solution.py:14
  121.2 11.0 %all-to-all-start = ((bf16[8,128,192]{1,2,0:T(8,128)(2,1)}), bf16[8,128,192]{1,2,0:T(8,128)(2,1)S(1)}, u32[]{:S(2)}, u32[]{:S(2)}) async-start(bf16[8,128,192]{1,2,0:T(8,128)(2,1)} %copy_bitcast_fusion), calls=%async_computation.1 | async-start | bytes 786432 | tf_op jit(solution)/shard_map/all_to_all | solution.py:40
  133.4 14.6 %all-to-all-start.1 = ((f32[8,1,512]{2,1,0:T(1,128)}), f32[8,1,512]{2,1,0:T(1,128)S(1)}, u32[]{:S(2)}, u32[]{:S(2)}) async-start(f32[8,1,512]{2,1,0:T(1,128)} %broadcast_in_dim.7), calls=%async_computation.2 | async-start | bytes 32768 | tf_op jit(solution)/shard_map/all_to_all | solution.py:19
  148.4 11.8 %collective-permute-start.1 = (bf16[128,1536]{0,1:T(8,128)(2,1)S(1)}, bf16[128,1536]{0,1:T(8,128)(2,1)S(1)}, u32[]{:S(2)}, u32[]{:S(2)}) collective-permute-start(bf16[128,1536]{0,1:T(8,128)(2,1)S(1)} %fusion.8), channel_id=1, source_target_pairs={{0,704},{64,0},{128,64},{192,128},{256,192},{320,256},{384,320},{4... | collective-permute-start | bytes 1179656 | tf_op jit(solution)/shard_map/ppermute | solution.py:14
Sparse Core Ops, SparseCore 0:
  14.9 90.5 reduce-scatter.1
where the time goes:
time: 168 us
  waiting for transfers between devices  121 us (72%)
  starting transfers between devices  16.3 us (10%)
  between operations  14.1 us (8%)
  matrix products  5.87 us (3%)
  other arithmetic  5.37 us (3%)
  local copies, waits for them, and re-layouts  5.15 us (3%)
    reduce_scatter x1, waiting for transfers between devices, local(): lax.psum_scatter(jnp.einsum('th,hjr->jtr', local_ctx, weights, preferred_...  90.7 us
    ppermute x2, waiting for transfers between devices, passed_along(): lax.ppermute(x, axis, [(i, (i + by) % devices) for i in range(devices)])  17.8 us
    all_to_all x1, starting transfers between devices, from_everyone(): return lax.all_to_all(copies, axis, split_axis=0, concat_axis=0, tiled=True)  7.54 us
    all_to_all x1, waiting for transfers between devices, relayout(): return lax.all_to_all(values, 'dp', split_axis=0, concat_axis=1, tiled=True)  7.28 us
    dot_general x1, matrix products, local(): jnp.einsum('th,hjr->jtr', local_ctx, weights, preferred_element_type=jnp....  5.87 us
    all_to_all x1, waiting for transfers between devices, from_everyone(): return lax.all_to_all(copies, axis, split_axis=0, concat_axis=0, tiled=True)  5.42 us
    ppermute x2, starting transfers between devices, passed_along(): lax.ppermute(x, axis, [(i, (i + by) % devices) for i in range(devices)])  5.27 us
    unnamed x11, local copies, waits for them, and re-layouts  3.71 us
  transfers between devices with their start and end apart: 5, of which 5 were waited for; matrix products, arithmetic and copies ran while one was open for 3% of the time, Pallas kernels for 0%

commit v1 on v0

v1 whole, which is shorter than its diff:
```python
import jax
import jax.numpy as jnp
from jax import lax
from jax.experimental import pallas as pl
from jax.experimental.pallas import tpu as pltpu
from jax.sharding import PartitionSpec as P

D = 12288
EPS = 1e-05
F32 = jnp.float32
BF16 = jnp.bfloat16
TB = 128
STEP = 2
ORDER = (2, 1, 3, 0)


def swap_core(x):
    n = lax.axis_size("mp")
    return lax.ppermute(x, "mp", [(i, i ^ 1) for i in range(n)])


def swap_y(x, pair):
    n = lax.axis_size("mp")
    return lax.ppermute(x, "mp", [(i, i ^ (2 * pair)) for i in range(n)])


def along_section(x, by):
    n = lax.axis_size("section")
    return lax.ppermute(x, "section", [(i, (i + by) % n) for i in range(n)])


def dot_t(w, c):
    return lax.dot_general(w, c, (((1,), (1,)), ((), ())), preferred_element_type=F32)


def params(mib):
    return pltpu.CompilerParams(vmem_limit_bytes=mib * 1024 * 1024)


def vmem(n):
    return [pl.BlockSpec(memory_space=pltpu.VMEM)] * n


def cost(n, rows, depth, toks):
    return pl.CostEstimate(flops=2 * n * rows * depth * toks, bytes_accessed=2 * n * rows * (depth + 2 * toks) + 2 * toks * depth, transcendentals=0)


def far_product(me, weights, ctx):
    n_blocks, rows, depth = weights.shape
    toks = ctx.shape[0]
    n_parts = 4

    def body(me_ref, w_ref, c_ref, far_ref, ctx_ref, near_w_ref, own_w_ref, far_w, c_sem, w_sem, own_sem):
        me = me_ref[0]
        core = me & 1

        def block(k, c):
            return (((me >> 1) ^ ORDER[k]) << 1) + c

        def c_copy(i):
            part = pl.ds(i * (toks // n_parts), toks // n_parts)
            return pltpu.make_async_copy(c_ref.at[part], ctx_ref.at[part], c_sem.at[i])

        def w_copy(k):
            to = far_w if k == 0 else near_w_ref.at[pl.ds((k - 1) * rows, rows)]
            return pltpu.make_async_copy(w_ref.at[block(k, 1 - core)], to, w_sem.at[k])

        def own_copy(k):
            return pltpu.make_async_copy(w_ref.at[block(k, core)], own_w_ref.at[pl.ds(k * rows, rows)], own_sem.at[k])

        w_copy(0).start()
        for i in range(n_parts):
            c_copy(i).start()
        for k in range(1, 4):
            w_copy(k).start()
        for k in range(4):
            own_copy(k).start()
        w_copy(0).wait()
        for i in range(n_parts):
            c_copy(i).wait()
        for i in range(toks // (STEP * TB)):
            acc = dot_t(far_w[...], ctx_ref[pl.ds(i * STEP * TB, STEP * TB)])
            for b in range(STEP):
                far_ref[STEP * i + b] = acc[:, b * TB:(b + 1) * TB].astype(BF16)
        for k in range(1, 4):
            w_copy(k).wait()
        for k in range(4):
            own_copy(k).wait()

    return pl.pallas_call(
        body,
        in_specs=[pl.BlockSpec(memory_space=pltpu.SMEM), pl.BlockSpec(memory_space=pltpu.HBM), pl.BlockSpec(memory_space=pltpu.HBM)],
        out_specs=vmem(4),
        out_shape=(
            jax.ShapeDtypeStruct((toks // TB, rows, TB), BF16),
            jax.ShapeDtypeStruct((toks, depth), BF16),
            jax.ShapeDtypeStruct((3 * rows, depth), BF16),
            jax.ShapeDtypeStruct((4 * rows, depth), BF16),
        ),
        scratch_shapes=[pltpu.VMEM((rows, depth), BF16), pltpu.SemaphoreType.DMA((n_parts,)), pltpu.SemaphoreType.DMA((4,)), pltpu.SemaphoreType.DMA((4,))],
        compiler_params=params(16), cost_estimate=cost(1, rows, depth, toks), name="far_product",
    )(me, weights, ctx)


def near_product(weights, ctx):
    toks, depth = ctx.shape
    rows = weights.shape[0] // 3

    def body(w_ref, c_ref, o_ref):
        for i in range(toks // (STEP * TB)):
            acc = dot_t(w_ref[...], c_ref[pl.ds(i * STEP * TB, STEP * TB)])
            for b in range(STEP):
                for k in range(3):
                    o_ref[k, STEP * i + b] = acc[k * rows:(k + 1) * rows, b * TB:(b + 1) * TB].astype(BF16)

    return pl.pallas_call(
        body, in_specs=vmem(2), out_specs=vmem(1)[0], out_shape=jax.ShapeDtypeStruct((3, toks // TB, rows, TB), BF16),
        compiler_params=params(16), cost_estimate=cost(3, rows, depth, toks), name="near_product",
    )(weights, ctx)


def far_sum(weights, ctx, other):
    toks, depth = ctx.shape
    rows = weights.shape[0] // 4
    half = rows // 2

    def body(w_ref, c_ref, r_ref, top_ref, low_ref):
        for i in range(toks // (STEP * TB)):
            acc = dot_t(w_ref[:rows], c_ref[pl.ds(i * STEP * TB, STEP * TB)])
            for b in range(STEP):
                total = (acc[:, b * TB:(b + 1) * TB] + r_ref[STEP * i + b].astype(F32)).astype(BF16)
                top_ref[STEP * i + b] = total[:half]
                low_ref[STEP * i + b] = total[half:]

    shape = jax.ShapeDtypeStruct((toks // TB, half, TB), BF16)
    return pl.pallas_call(
        body, in_specs=vmem(3), out_specs=vmem(2), out_shape=(shape, shape),
        compiler_params=params(16), cost_estimate=cost(1, rows, depth, toks), name="far_sum",
    )(weights, ctx, other)


def near_sum(weights, ctx, other, residual, cot, gain):
    toks, depth = ctx.shape
    rows = weights.shape[0] // 4
    half = rows // 2
    width = cot.shape[1]

    def body(w_ref, c_ref, r_ref, res_ref, cot_ref, gain_ref, one_ref, three_ref, keep_one_ref, keep_three_ref, mine_ref, pack_ref):
        pack_ref[:TB] = cot_ref[...]
        g = gain_ref[...]
        hi = g.astype(BF16)
        g = g - hi.astype(F32)
        mid = g.astype(BF16)
        low = (g - mid.astype(F32)).astype(BF16)
        row = lax.broadcasted_iota(jnp.int32, (16, width), 0)
        parts = jnp.where(row == 0, hi.astype(F32), jnp.where(row == 1, mid.astype(F32), jnp.where(row == 2, low.astype(F32), 0.0)))
        pack_ref[TB:] = parts.astype(BF16)
        for i in range(toks // (STEP * TB)):
            acc = dot_t(w_ref[rows:], c_ref[pl.ds(i * STEP * TB, STEP * TB)])
            for b in range(STEP):
                t = STEP * i + b
                cut = slice(b * TB, (b + 1) * TB)
                one = acc[:rows, cut] + r_ref[0, t].astype(F32)
                one_ref[t] = one[:half].astype(BF16)
                keep_one_ref[t] = one[half:]
                three = acc[rows:2 * rows, cut] + r_ref[1, t].astype(F32)
                three_ref[t] = three[half:].astype(BF16)
                keep_three_ref[t] = three[:half]
                mine_ref[t] = acc[2 * rows:, cut] + r_ref[2, t].astype(F32) + res_ref[:, t * TB:(t + 1) * TB].astype(F32)

    part = lambda dtype: jax.ShapeDtypeStruct((toks // TB, half, TB), dtype)
    return pl.pallas_call(
        body, in_specs=vmem(6), out_specs=vmem(6),
        out_shape=(part(BF16), part(BF16), part(F32), part(F32), jax.ShapeDtypeStruct((toks // TB, rows, TB), F32), jax.ShapeDtypeStruct((TB + 16, width), BF16)),
        compiler_params=params(20), cost_estimate=cost(3, rows, depth, toks), name="near_sum",
    )(weights, ctx, other, residual, cot, gain)


def add_halves(mine, top, low, dtype, name):
    half = top.shape[1]

    def body(mine_ref, top_ref, low_ref, o_ref):
        o_ref[:, :half] = (mine_ref[:, :half] + top_ref[...].astype(F32)).astype(dtype)
        o_ref[:, half:] = (mine_ref[:, half:] + low_ref[...].astype(F32)).astype(dtype)

    return pl.pallas_call(
        body, in_specs=vmem(3), out_specs=vmem(1)[0], out_shape=jax.ShapeDtypeStruct(mine.shape, dtype), name=name, compiler_params=params(8),
        cost_estimate=pl.CostEstimate(flops=mine.size, bytes_accessed=9 * mine.size, transcendentals=0),
    )(mine, top, low)


def relay_sum(keep_one, keep_three, from_one, from_three):
    def body(keep_one_ref, keep_three_ref, from_one_ref, from_three_ref, one_ref, three_ref):
        one_ref[...] = (keep_one_ref[...] + from_three_ref[...].astype(F32)).astype(BF16)
        three_ref[...] = (keep_three_ref[...] + from_one_ref[...].astype(F32)).astype(BF16)

    shape = jax.ShapeDtypeStruct(keep_one.shape, BF16)
    return pl.pallas_call(
        body, in_specs=vmem(4), out_specs=vmem(2), out_shape=(shape, shape), name="relay_sum", compiler_params=params(8),
        cost_estimate=pl.CostEstimate(flops=2 * keep_one.size, bytes_accessed=16 * keep_one.size, transcendentals=0),
    )(keep_one, keep_three, from_one, from_three)


def over_mp(x):
    n = lax.axis_size("mp")
    return jnp.sum(lax.all_to_all(jnp.broadcast_to(x, (n, *x.shape)), "mp", split_axis=0, concat_axis=0, tiled=True), axis=0)


def local(context, out_weight, residual, gain, bias, cot):
    m = lax.axis_index("mp").astype(jnp.int32)
    weights = out_weight[0][:, :, 0, :].transpose(1, 2, 0)
    weights = pltpu.with_memory_space_constraint(weights, pltpu.HBM)
    ctx = pltpu.with_memory_space_constraint(context[0], pltpu.HBM)

    far_sent, ctx, near_weights, own_weights = far_product(m.reshape(1), weights, ctx)
    far_got = swap_core(far_sent)
    near_got = swap_core(near_product(near_weights, ctx))
    far_top, far_low = far_sum(own_weights, ctx, far_got)
    relay_one = swap_y(far_top, 1)
    relay_three = swap_y(far_low, 3)
    one, three, keep_one, keep_three, mine, pack = near_sum(own_weights, ctx, near_got, residual[0].T, cot[0], gain)
    direct_one = swap_y(one, 1)
    direct_three = swap_y(three, 3)
    on_one, on_three = relay_sum(keep_one, keep_three, relay_one, relay_three)
    sum_one = swap_y(on_one, 1)
    sum_three = swap_y(on_three, 3)
    pack_next = along_section(pack, -1)
    mine = add_halves(mine, direct_one, direct_three, F32, "add_direct")
    section_out = add_halves(mine, sum_three, sum_one, BF16, "add_last")
    got = lax.all_to_all(section_out, "dp", split_axis=0, concat_axis=0, tiled=True)

    parts = pack_next[TB:TB + 3].astype(F32)
    gain_next = parts[0:1] + parts[1:2] + parts[2:3]
    scaled = pack_next[:TB].astype(F32) * gain_next
    width = float(D)

    got_next = along_section(got, 1)
    x = got.reshape(-1, TB).T.astype(F32)
    sums = jnp.stack([jnp.sum(x, -1), jnp.sum(x * x, -1), jnp.sum(scaled, -1), jnp.sum(scaled * x, -1)])
    sums = over_mp(sums)
    average = sums[0] / width
    rstd = lax.rsqrt(sums[1] / width - average * average + EPS)
    first = sums[2] / width
    second = rstd * (sums[3] / width - average * first)
    ar_next = along_section(jnp.stack([average, rstd]), 1)
    xhat = (x - average[:, None]) * rstd[:, None]
    grad = (rstd[:, None] * (scaled - first[:, None] - xhat * second[:, None])).astype(BF16)
    xn = got_next.reshape(-1, TB).T.astype(F32)
    out = ((xn - ar_next[0][:, None]) * ar_next[1][:, None] * gain + bias).astype(BF16)
    return out[None], grad[None]


def solution(mesh):
    in_specs = (
        P("section", None, "mp"),
        P("section", "mp", None, "dp", None),
        P("section", None, ("mp", "dp")),
        P("section", "mp"),
        P("section", "mp"),
        P("section", "dp", "mp"),
    )
    out_specs = (P("section", "dp", "mp"), P("section", "dp", "mp"))
    return jax.shard_map(local, mesh=mesh, in_specs=in_specs, out_specs=out_specs, check_vma=False)
```

time: 168 us -> 98.9 us (0.59)
  waiting for transfers between devices: 121 us -> 29.4 us
  starting transfers between devices: 16.3 us -> 57.6 us
  between operations: 14.1 us -> 0.89 us
  Pallas kernels: 0 us -> 6.6 us
  matrix products: 5.87 us -> 0 us
  local copies, waits for them, and re-layouts: 5.15 us -> 1.08 us
  other arithmetic: 5.37 us -> 2.74 us
    reduce_scatter x1 -> x0, waiting for transfers between devices: 90.7 us -> none  [local(): lax.psum_scatter(jnp.einsum('th,hjr->jtr', local_ctx, weights, preferred_...]
    ppermute x2 -> x11, starting transfers between devices: 5.27 us -> 46.7 us  [the longest x6 17.4 us: swap_y(): return lax.ppermute(x, 'mp', [(i, i ^ 2 * pair) for i in range(n)])]
    pallas_call x0 -> x7, Pallas kernels: none -> 6.6 us  [the longest x1 2.67 us: far_product(): pl.pallas_call(body, in_specs=[pl.BlockSpec(memory_space=pltpu.SMEM), pl....]
    dot_general x1 -> x0, matrix products: 5.87 us -> none  [local(): jnp.einsum('th,hjr->jtr', local_ctx, weights, preferred_element_type=jnp....]
    convert_element_type x4 -> x2, other arithmetic: 4.08 us -> 0.08 us  [the longest x1 0.08 us: local(): xn = got_next.reshape(-1, TB).T.astype(F32)]
    unnamed x11 -> x8, local copies, waits for them, and re-layouts: 3.71 us -> 0.01 us
    broadcast_in_dim x0 -> x2, other arithmetic: none -> 2.01 us  [local(): return (out[None], grad[None])]
    ppermute x2 -> x11, waiting for transfers between devices: 17.8 us -> 17 us  [the longest x6 11.5 us: swap_y(): return lax.ppermute(x, 'mp', [(i, i ^ 2 * pair) for i in range(n)])]
  transfers between devices with their start and end apart: 5 -> 13, of which waited for: 5 -> 6; matrix products, arithmetic and copies ran while one was open for 3% -> 1% of each run, Pallas kernels for 0% -> 3%
where the time goes in v1:
time: 98.9 us; the launch traced here: 98.3 us
  starting transfers between devices  57.6 us (58%)
  waiting for transfers between devices  29.4 us (30%)
  Pallas kernels  6.6 us (7%)
  other arithmetic  2.74 us (3%)
  local copies, waits for them, and re-layouts  1.08 us (1%)
    ppermute x6, starting transfers between devices, swap_y(): return lax.ppermute(x, 'mp', [(i, i ^ 2 * pair) for i in range(n)])  17.4 us
    ppermute x3, starting transfers between devices, along_section(): return lax.ppermute(x, 'section', [(i, (i + by) % n) for i in range(n)])  14.9 us
    ppermute x2, starting transfers between devices, swap_core(): return lax.ppermute(x, 'mp', [(i, i ^ 1) for i in range(n)])  14.3 us
    ppermute x6, waiting for transfers between devices, swap_y(): return lax.ppermute(x, 'mp', [(i, i ^ 2 * pair) for i in range(n)])  11.5 us
    all_to_all x1, waiting for transfers between devices, local(): lax.all_to_all(section_out, 'dp', split_axis=0, concat_axis=0, tiled=True)  7.34 us
    all_to_all x1, starting transfers between devices, over_mp(): lax.all_to_all(jnp.broadcast_to(x, (n, *x.shape)), 'mp', split_axis=0, co...  6.89 us
    all_to_all x1, waiting for transfers between devices, over_mp(): lax.all_to_all(jnp.broadcast_to(x, (n, *x.shape)), 'mp', split_axis=0, co...  5.07 us
    all_to_all x1, starting transfers between devices, local(): lax.all_to_all(section_out, 'dp', split_axis=0, concat_axis=0, tiled=True)  4 us
  transfers between devices with their start and end apart: 13, of which 6 were waited for; matrix products, arithmetic and copies ran while one was open for 1% of the time, Pallas kernels for 3%

profile of v1, /device:TPU:1, one launch (start us, length us, event | category | flops | bytes accessed | tf_op | source)
XLA Modules:
  0.0 98.3 jit_solution(2604628994280748544)
XLA Ops:
  0.6 2.7 %far_product.1 = (bf16[8,192,128]{2,1,0:T(8,128)(2,1)S(1)}, bf16[1024,768]{1,0:T(8,128)(2,1)S(1)}, bf16[576,768]{1,0:T(8,128)(2,1)S(1)}, bf16[768,768]{1,0:T(8,128)(2,1)S(1)}) custom-call(s32[1]{0:T(128)} %bitcast.me_ref, bf16[8,192,768]{2,1,0:T(8,128)(2,1)} %bitcast.73, bf16[1024,768]{1,0:T(8,128)(2,1)} %bitcast.74), custom_call_target="tpu_custom_call" | custom-call | flops 301989888 | bytes 2654208 | tf_op jit(solution)/shard_map/far_product/pallas_call | solution.py:90
  3.3 1.1 %near_product.1 = bf16[3,8,192,128]{3,2,1,0:T(8,128)(2,1)S(1)} custom-call(bf16[576,768]{1,0:T(8,128)(2,1)S(1)} %get-tuple-element.18.w_ref, bf16[1024,768]{1,0:T(8,128)(2,1)S(1)} %get-tuple-element.17.c_ref), custom_call_target="tpu_custom_call" | custom-call | flops 905969664 | bytes 4816896 | tf_op jit(solution)/shard_map/near_product/pallas_call | solution.py:116
  4.4 12.4 %collective-permute-start = (bf16[3,8,192,128]{3,2,1,0:T(8,128)(2,1)S(1)}, bf16[3,8,192,128]{3,2,1,0:T(8,128)(2,1)S(1)}, u32[]{:S(2)}, u32[]{:S(2)}) collective-permute-start(bf16[3,8,192,128]{3,2,1,0:T(8,128)(2,1)S(1)} %near_product.1), channel_id=1, source_target_pairs={{0,8},{8,0},{16,24},{24,16},{32,40},{40,32},{48,56},{56,48},{1,9},... | collective-permute-start | bytes 3538952 | tf_op jit(solution)/shard_map/ppermute | solution.py:19
  16.9 1.9 %collective-permute-start.3 = (bf16[8,192,128]{2,1,0:T(8,128)(2,1)S(1)}, bf16[8,192,128]{2,1,0:T(8,128)(2,1)S(1)}, u32[]{:S(2)}, u32[]{:S(2)}) collective-permute-start(bf16[8,192,128]{2,1,0:T(8,128)(2,1)S(1)} %get-tuple-element.24), channel_id=1, source_target_pairs={{0,8},{8,0},{16,24},{24,16},{32,40},{40,32},{48,56},{56,48},{1,9},... | collective-permute-start | bytes 1179656 | tf_op jit(solution)/shard_map/ppermute | solution.py:19
  18.8 1.7 %collective-permute-done.3.r_ref = bf16[8,192,128]{2,1,0:T(8,128)(2,1)S(1)} collective-permute-done((bf16[8,192,128]{2,1,0:T(8,128)(2,1)S(1)}, bf16[8,192,128]{2,1,0:T(8,128)(2,1)S(1)}, u32[]{:S(2)}, u32[]{:S(2)}) %collective-permute-start.3) | collective-permute-done | bytes 393248 | tf_op jit(solution)/shard_map/ppermute | solution.py:19
  20.5 0.0 copy-start
  20.5 0.0 copy-start.1
  20.5 0.0 copy-start.2
  20.5 0.7 far_sum.1
  21.2 1.9 %collective-permute-start.4 = (bf16[8,96,128]{2,1,0:T(8,128)(2,1)S(1)}, bf16[8,96,128]{2,1,0:T(8,128)(2,1)S(1)}, u32[]{:S(2)}, u32[]{:S(2)}) collective-permute-start(bf16[8,96,128]{2,1,0:T(8,128)(2,1)S(1)} %get-tuple-element.25), channel_id=1, source_target_pairs={{0,16},{8,24},{16,0},{24,8},{32,48},{40,56},{48,32},{56,40},{1,17}... | collective-permute-start | bytes 589832 | tf_op jit(solution)/shard_map/ppermute | solution.py:24
  23.1 1.9 %collective-permute-start.5 = (bf16[8,96,128]{2,1,0:T(8,128)(2,1)S(1)}, bf16[8,96,128]{2,1,0:T(8,128)(2,1)S(1)}, u32[]{:S(2)}, u32[]{:S(2)}) collective-permute-start(bf16[8,96,128]{2,1,0:T(8,128)(2,1)S(1)} %get-tuple-element.26), channel_id=1, source_target_pairs={{0,48},{8,56},{16,32},{24,40},{32,16},{40,24},{48,0},{56,8},{1,49}... | collective-permute-start | bytes 589832 | tf_op jit(solution)/shard_map/ppermute | solution.py:24
  25.0 0.0 collective-permute-done.r_ref
  25.0 0.0 copy-done
  25.0 0.0 copy-done.1
  25.1 0.0 copy-done.2
  25.1 1.1 %near_sum.1 = (bf16[8,96,128]{2,1,0:T(8,128)(2,1)S(1)}, bf16[8,96,128]{2,1,0:T(8,128)(2,1)S(1)}, f32[8,96,128]{2,1,0:T(8,128)S(1)}, f32[8,96,128]{2,1,0:T(8,128)...) custom-call(bf16[768,768]{1,0:T(8,128)(2,1)S(1)} %get-tuple-element.16.w_ref, ...), custom_call_target="tpu_custom_call" | custom-call | flops 905969664 | bytes 4816896 | tf_op jit(solution)/shard_map/near_sum/pallas_call | solution.py:172
  26.2 11.1 %collective-permute-start.9 = (bf16[144,1536]{1,0:T(8,128)(2,1)S(1)}, bf16[144,1536]{1,0:T(8,128)(2,1)S(1)}, u32[]{:S(2)}, u32[]{:S(2)}) collective-permute-start(bf16[144,1536]{1,0:T(8,128)(2,1)S(1)} %get-tuple-element.29), channel_id=1, source_target_pairs={{0,704},{64,0},{128,64},{192,128},{256,192},{320,256},{384,320},{4... | collective-permute-start | bytes 1327112 | tf_op jit(solution)/shard_map/ppermute | solution.py:29
  37.3 2.4 %collective-permute-start.1 = (bf16[8,96,128]{2,1,0:T(8,128)(2,1)S(1)}, bf16[8,96,128]{2,1,0:T(8,128)(2,1)S(1)}, u32[]{:S(2)}, u32[]{:S(2)}) collective-permute-start(bf16[8,96,128]{2,1,0:T(8,128)(2,1)S(1)} %get-tuple-element.20), channel_id=1, source_target_pairs={{0,16},{8,24},{16,0},{24,8},{32,48},{40,56},{48,32},{56,40},{1,17}... | collective-permute-start | bytes 589832 | tf_op jit(solution)/shard_map/ppermute | solution.py:24
  39.8 1.9 %collective-permute-start.2 = (bf16[8,96,128]{2,1,0:T(8,128)(2,1)S(1)}, bf16[8,96,128]{2,1,0:T(8,128)(2,1)S(1)}, u32[]{:S(2)}, u32[]{:S(2)}) collective-permute-start(bf16[8,96,128]{2,1,0:T(8,128)(2,1)S(1)} %get-tuple-element.21), channel_id=1, source_target_pairs={{0,48},{8,56},{16,32},{24,40},{32,16},{40,24},{48,0},{56,8},{1,49}... | collective-permute-start | bytes 589832 | tf_op jit(solution)/shard_map/ppermute | solution.py:24
  41.7 0.0 collective-permute-done.4.from_one_ref
  41.7 0.0 collective-permute-done.5.from_three_ref
  41.7 0.1 relay_sum.1
  41.8 5.5 %collective-permute-start.6 = (bf16[8,96,128]{2,1,0:T(8,128)(2,1)S(1)}, bf16[8,96,128]{2,1,0:T(8,128)(2,1)S(1)}, u32[]{:S(2)}, u32[]{:S(2)}) collective-permute-start(bf16[8,96,128]{2,1,0:T(8,128)(2,1)S(1)} %get-tuple-element.27), channel_id=1, source_target_pairs={{0,48},{8,56},{16,32},{24,40},{32,16},{40,24},{48,0},{56,8},{1,49}... | collective-permute-start | bytes 589832 | tf_op jit(solution)/shard_map/ppermute | solution.py:24
  47.3 3.8 %collective-permute-start.7 = (bf16[8,96,128]{2,1,0:T(8,128)(2,1)S(1)}, bf16[8,96,128]{2,1,0:T(8,128)(2,1)S(1)}, u32[]{:S(2)}, u32[]{:S(2)}) collective-permute-start(bf16[8,96,128]{2,1,0:T(8,128)(2,1)S(1)} %get-tuple-element.28), channel_id=1, source_target_pairs={{0,16},{8,24},{16,0},{24,8},{32,48},{40,56},{48,32},{56,40},{1,17}... | collective-permute-start | bytes 589832 | tf_op jit(solution)/shard_map/ppermute | solution.py:24
  51.1 0.0 collective-permute-done.1.top_ref
  51.1 4.9 %collective-permute-done.2.low_ref = bf16[8,96,128]{2,1,0:T(8,128)(2,1)S(1)} collective-permute-done((bf16[8,96,128]{2,1,0:T(8,128)(2,1)S(1)}, bf16[8,96,128]{2,1,0:T(8,128)(2,1)S(1)}, u32[]{:S(2)}, u32[]{:S(2)}) %collective-permute-start.2) | collective-permute-done | bytes 196640 | tf_op jit(solution)/shard_map/ppermute | solution.py:24
  56.0 0.1 add_direct.1.mine_ref
  56.1 6.5 %collective-permute-done.6.top_ref = bf16[8,96,128]{2,1,0:T(8,128)(2,1)S(1)} collective-permute-done((bf16[8,96,128]{2,1,0:T(8,128)(2,1)S(1)}, bf16[8,96,128]{2,1,0:T(8,128)(2,1)S(1)}, u32[]{:S(2)}, u32[]{:S(2)}) %collective-permute-start.6) | collective-permute-done | bytes 196640 | tf_op jit(solution)/shard_map/ppermute | solution.py:24
  62.7 0.0 collective-permute-done.7.low_ref
  62.7 0.8 add_last.1
  63.5 4.0 %all-to-all-start = ((bf16[8,192,128]{2,1,0:T(8,128)(2,1)}), bf16[8,192,128]{2,1,0:T(8,128)(2,1)S(1)}, u32[]{:S(2)}, u32[]{:S(2)}) async-start(bf16[8,192,128]{2,1,0:T(8,128)(2,1)} %add_last.1), calls=%async_computation | async-start | bytes 786432 | tf_op jit(solution)/shard_map/all_to_all | solution.py:230
  67.5 0.0 copy-start.3
  67.5 0.0 collective-permute-done.9
  67.5 7.3 %all-to-all-done = bf16[8,192,128]{2,1,0:T(8,128)(2,1)S(1)} async-done(((bf16[8,192,128]{2,1,0:T(8,128)(2,1)}), bf16[8,192,128]{2,1,0:T(8,128)(2,1)S(1)}, u32[]{:S(2)}, u32[]{:S(2)}) %all-to-all-start) | async-done | bytes 393248 | tf_op jit(solution)/shard_map/all_to_all | solution.py:230
  74.9 0.2 copy.12
  75.1 0.2 convert_reduce_fusion
  75.3 0.3 fusion
  75.6 0.6 broadcast_in_dim.6
  76.2 6.9 %all-to-all-start.1 = ((f32[8,4,128]{2,1,0:T(4,128)}), f32[8,4,128]{2,1,0:T(4,128)S(1)}, u32[]{:S(2)}, u32[]{:S(2)}) async-start(f32[8,4,128]{2,1,0:T(4,128)} %broadcast_in_dim.6), calls=%async_computation.1 | async-start | bytes 32768 | tf_op jit(solution)/shard_map/all_to_all | solution.py:206
  83.1 0.0 copy-done.3
  83.2 1.9 %collective-permute-start.8 = (bf16[8,192,128]{2,1,0:T(8,128)(2,1)S(1)}, bf16[8,192,128]{2,1,0:T(8,128)(2,1)S(1)}, u32[]{:S(2)}, u32[]{:S(2)}) collective-permute-start(bf16[8,192,128]{2,1,0:T(8,128)(2,1)S(1)} %all-to-all-done), channel_id=1, source_target_pairs={{0,64},{64,128},{128,192},{192,256},{256,320},{320,384},{384,448},... | collective-permute-start | bytes 1179656 | tf_op jit(solution)/shard_map/ppermute | solution.py:29
  85.1 5.1 %all-to-all-done.1 = f32[8,4,128]{2,1,0:T(4,128)S(1)} async-done(((f32[8,4,128]{2,1,0:T(4,128)}), f32[8,4,128]{2,1,0:T(4,128)S(1)}, u32[]{:S(2)}, u32[]{:S(2)}) %all-to-all-start.1) | async-done | bytes 16416 | tf_op jit(solution)/shard_map/all_to_all | solution.py:206
  90.2 1.9 %collective-permute-start.10 = (f32[2,128]{1,0:T(2,128)S(1)}, f32[2,128]{1,0:T(2,128)S(1)}, u32[]{:S(2)}, u32[]{:S(2)}) collective-permute-start(f32[2,128]{1,0:T(2,128)S(1)} %pad_maximum_fusion.1), channel_id=1, source_target_pairs={{0,64},{64,128},{128,192},{192,256},{256,320},{320,384},{384,448},... | collective-permute-start | bytes 3080 | tf_op jit(solution)/shard_map/ppermute | solution.py:29
  92.2 1.1 %fusion.9 = bf16[1,128,1536]{2,1,0:T(8,128)(2,1)} fusion(f32[1536,128]{0,1:T(8,128)S(1)} %copy.12, f32[128]{0:T(128)S(1)} %get-tuple-element.34, f32[128]{0:T(128)S(1)} %get-tuple-element.36, f32[128]{0:T(128)S(1)} %get-tuple-element.35, f32[128]{0:T(128)S(1)} %get-tuple-element.33, f32[1536]{0:T(1024)S(1)} %fusion.10, ...), kind=kLoop, calls=%fused_computation.14 | loop fusion | flops 1769472 | bytes 1581056 | tf_op jit(solution)/shard_map/broadcast_in_dim | solution.py:250
  93.2 3.8 %collective-permute-done.10 = f32[2,128]{1,0:T(2,128)S(1)} collective-permute-done((f32[2,128]{1,0:T(2,128)S(1)}, f32[2,128]{1,0:T(2,128)S(1)}, u32[]{:S(2)}, u32[]{:S(2)}) %collective-permute-start.10) | collective-permute-done | bytes 1056 | tf_op jit(solution)/shard_map/ppermute | solution.py:29
  97.0 0.0 collective-permute-done.8
  97.0 0.1 bitcast_convert_fusion
  97.1 0.3 copy.14
  97.4 0.9 fusion.8
  (10 shorter events, 0.1 us)
Async XLA Ops:
  4.4 20.6 %collective-permute-start = (bf16[3,8,192,128]{3,2,1,0:T(8,128)(2,1)S(1)}, bf16[3,8,192,128]{3,2,1,0:T(8,128)(2,1)S(1)}, u32[]{:S(2)}, u32[]{:S(2)}) collective-permute-start(bf16[3,8,192,128]{3,2,1,0:T(8,128)(2,1)S(1)} %near_product.1), channel_id=1, source_target_pairs={{0,8},{8,0},{16,24},{24,16},{32,40},{40,32},{48,56},{56,48},{1,9},... | collective-permute-start | bytes 3538952 | tf_op jit(solution)/shard_map/ppermute | solution.py:19
  16.9 3.6 %collective-permute-start.3 = (bf16[8,192,128]{2,1,0:T(8,128)(2,1)S(1)}, bf16[8,192,128]{2,1,0:T(8,128)(2,1)S(1)}, u32[]{:S(2)}, u32[]{:S(2)}) collective-permute-start(bf16[8,192,128]{2,1,0:T(8,128)(2,1)S(1)} %get-tuple-element.24), channel_id=1, source_target_pairs={{0,8},{8,0},{16,24},{24,16},{32,40},{40,32},{48,56},{56,48},{1,9},... | collective-permute-start | bytes 1179656 | tf_op jit(solution)/shard_map/ppermute | solution.py:19
  20.5 4.6 %copy-start = (bf16[1,1024,192]{1,2,0:T(8,128)(2,1)S(1)}, bf16[1,1024,192]{1,2,0:T(8,128)(2,1)}, u32[]{:S(2)}) copy-start(bf16[1,1024,192]{1,2,0:T(8,128)(2,1)} %param.8) | copy-start | bytes 1179652
  20.5 4.6 %copy-start.1 = (bf16[1,128,1536]{2,1,0:T(8,128)(2,1)S(1)}, bf16[1,128,1536]{2,1,0:T(8,128)(2,1)}, u32[]{:S(2)}) copy-start(bf16[1,128,1536]{2,1,0:T(8,128)(2,1)} %param.11) | copy-start | bytes 1179652
  20.5 4.6 %copy-start.2 = (f32[1,1536]{1,0:T(1,128)S(1)}, f32[1,1536]{1,0:T(1,128)}, u32[]{:S(2)}) copy-start(f32[1,1536]{1,0:T(1,128)} %gain_ref.1) | copy-start | bytes 18436
  21.2 20.5 %collective-permute-start.4 = (bf16[8,96,128]{2,1,0:T(8,128)(2,1)S(1)}, bf16[8,96,128]{2,1,0:T(8,128)(2,1)S(1)}, u32[]{:S(2)}, u32[]{:S(2)}) collective-permute-start(bf16[8,96,128]{2,1,0:T(8,128)(2,1)S(1)} %get-tuple-element.25), channel_id=1, source_target_pairs={{0,16},{8,24},{16,0},{24,8},{32,48},{40,56},{48,32},{56,40},{1,17}... | collective-permute-start | bytes 589832 | tf_op jit(solution)/shard_map/ppermute | solution.py:24
  23.1 18.6 %collective-permute-start.5 = (bf16[8,96,128]{2,1,0:T(8,128)(2,1)S(1)}, bf16[8,96,128]{2,1,0:T(8,128)(2,1)S(1)}, u32[]{:S(2)}, u32[]{:S(2)}) collective-permute-start(bf16[8,96,128]{2,1,0:T(8,128)(2,1)S(1)} %get-tuple-element.26), channel_id=1, source_target_pairs={{0,48},{8,56},{16,32},{24,40},{32,16},{40,24},{48,0},{56,8},{1,49}... | collective-permute-start | bytes 589832 | tf_op jit(solution)/shard_map/ppermute | solution.py:24
  26.2 41.3 %collective-permute-start.9 = (bf16[144,1536]{1,0:T(8,128)(2,1)S(1)}, bf16[144,1536]{1,0:T(8,128)(2,1)S(1)}, u32[]{:S(2)}, u32[]{:S(2)}) collective-permute-start(bf16[144,1536]{1,0:T(8,128)(2,1)S(1)} %get-tuple-element.29), channel_id=1, source_target_pairs={{0,704},{64,0},{128,64},{192,128},{256,192},{320,256},{384,320},{4... | collective-permute-start | bytes 1327112 | tf_op jit(solution)/shard_map/ppermute | solution.py:29
  37.3 13.8 %collective-permute-start.1 = (bf16[8,96,128]{2,1,0:T(8,128)(2,1)S(1)}, bf16[8,96,128]{2,1,0:T(8,128)(2,1)S(1)}, u32[]{:S(2)}, u32[]{:S(2)}) collective-permute-start(bf16[8,96,128]{2,1,0:T(8,128)(2,1)S(1)} %get-tuple-element.20), channel_id=1, source_target_pairs={{0,16},{8,24},{16,0},{24,8},{32,48},{40,56},{48,32},{56,40},{1,17}... | collective-permute-start | bytes 589832 | tf_op jit(solution)/shard_map/ppermute | solution.py:24
  39.8 16.3 %collective-permute-start.2 = (bf16[8,96,128]{2,1,0:T(8,128)(2,1)S(1)}, bf16[8,96,128]{2,1,0:T(8,128)(2,1)S(1)}, u32[]{:S(2)}, u32[]{:S(2)}) collective-permute-start(bf16[8,96,128]{2,1,0:T(8,128)(2,1)S(1)} %get-tuple-element.21), channel_id=1, source_target_pairs={{0,48},{8,56},{16,32},{24,40},{32,16},{40,24},{48,0},{56,8},{1,49}... | collective-permute-start | bytes 589832 | tf_op jit(solution)/shard_map/ppermute | solution.py:24
  41.8 20.9 %collective-permute-start.6 = (bf16[8,96,128]{2,1,0:T(8,128)(2,1)S(1)}, bf16[8,96,128]{2,1,0:T(8,128)(2,1)S(1)}, u32[]{:S(2)}, u32[]{:S(2)}) collective-permute-start(bf16[8,96,128]{2,1,0:T(8,128)(2,1)S(1)} %get-tuple-element.27), channel_id=1, source_target_pairs={{0,48},{8,56},{16,32},{24,40},{32,16},{40,24},{48,0},{56,8},{1,49}... | collective-permute-start | bytes 589832 | tf_op jit(solution)/shard_map/ppermute | solution.py:24
  47.3 15.4 %collective-permute-start.7 = (bf16[8,96,128]{2,1,0:T(8,128)(2,1)S(1)}, bf16[8,96,128]{2,1,0:T(8,128)(2,1)S(1)}, u32[]{:S(2)}, u32[]{:S(2)}) collective-permute-start(bf16[8,96,128]{2,1,0:T(8,128)(2,1)S(1)} %get-tuple-element.28), channel_id=1, source_target_pairs={{0,16},{8,24},{16,0},{24,8},{32,48},{40,56},{48,32},{56,40},{1,17}... | collective-permute-start | bytes 589832 | tf_op jit(solution)/shard_map/ppermute | solution.py:24
  63.5 11.4 %all-to-all-start = ((bf16[8,192,128]{2,1,0:T(8,128)(2,1)}), bf16[8,192,128]{2,1,0:T(8,128)(2,1)S(1)}, u32[]{:S(2)}, u32[]{:S(2)}) async-start(bf16[8,192,128]{2,1,0:T(8,128)(2,1)} %add_last.1), calls=%async_computation | async-start | bytes 786432 | tf_op jit(solution)/shard_map/all_to_all | solution.py:230
  67.5 15.7 %copy-start.3 = (f32[1,1536]{1,0:T(1,128)S(1)}, f32[1,1536]{1,0:T(1,128)}, u32[]{:S(2)}) copy-start(f32[1,1536]{1,0:T(1,128)} %param.10) | copy-start | bytes 18436
  76.2 14.0 %all-to-all-start.1 = ((f32[8,4,128]{2,1,0:T(4,128)}), f32[8,4,128]{2,1,0:T(4,128)S(1)}, u32[]{:S(2)}, u32[]{:S(2)}) async-start(f32[8,4,128]{2,1,0:T(4,128)} %broadcast_in_dim.6), calls=%async_computation.1 | async-start | bytes 32768 | tf_op jit(solution)/shard_map/all_to_all | solution.py:206
  83.2 13.9 %collective-permute-start.8 = (bf16[8,192,128]{2,1,0:T(8,128)(2,1)S(1)}, bf16[8,192,128]{2,1,0:T(8,128)(2,1)S(1)}, u32[]{:S(2)}, u32[]{:S(2)}) collective-permute-start(bf16[8,192,128]{2,1,0:T(8,128)(2,1)S(1)} %all-to-all-done), channel_id=1, source_target_pairs={{0,64},{64,128},{128,192},{192,256},{256,320},{320,384},{384,448},... | collective-permute-start | bytes 1179656 | tf_op jit(solution)/shard_map/ppermute | solution.py:29
  90.2 6.8 %collective-permute-start.10 = (f32[2,128]{1,0:T(2,128)S(1)}, f32[2,128]{1,0:T(2,128)S(1)}, u32[]{:S(2)}, u32[]{:S(2)}) collective-permute-start(f32[2,128]{1,0:T(2,128)S(1)} %pad_maximum_fusion.1), channel_id=1, source_target_pairs={{0,64},{64,128},{128,192},{192,256},{256,320},{320,384},{384,448},... | collective-permute-start | bytes 3080 | tf_op jit(solution)/shard_map/ppermute | solution.py:29

commit v2 on v1

--- a/solution.py
+++ b/solution.py
@@ -102,11 +102,11 @@
     )(me, weights, ctx)
 
 
-def near_product(weights, ctx):
+def near_product(weights, ctx, after):
     toks, depth = ctx.shape
     rows = weights.shape[0] // 3
 
-    def body(w_ref, c_ref, o_ref):
+    def body(w_ref, c_ref, after_ref, o_ref):
         for i in range(toks // (STEP * TB)):
             acc = dot_t(w_ref[...], c_ref[pl.ds(i * STEP * TB, STEP * TB)])
             for b in range(STEP):
@@ -114,9 +114,9 @@
                     o_ref[k, STEP * i + b] = acc[k * rows:(k + 1) * rows, b * TB:(b + 1) * TB].astype(BF16)
 
     return pl.pallas_call(
-        body, in_specs=vmem(2), out_specs=vmem(1)[0], out_shape=jax.ShapeDtypeStruct((3, toks // TB, rows, TB), BF16),
+        body, in_specs=[*vmem(2), pl.BlockSpec(memory_space=pl.ANY)], out_specs=vmem(1)[0], out_shape=jax.ShapeDtypeStruct((3, toks // TB, rows, TB), BF16),
         compiler_params=params(16), cost_estimate=cost(3, rows, depth, toks), name="near_product",
-    )(weights, ctx)
+    )(weights, ctx, after)
 
 
 def far_sum(weights, ctx, other):
@@ -139,22 +139,12 @@
     )(weights, ctx, other)
 
 
-def near_sum(weights, ctx, other, residual, cot, gain):
+def near_sum(weights, ctx, other, residual):
     toks, depth = ctx.shape
     rows = weights.shape[0] // 4
     half = rows // 2
-    width = cot.shape[1]
-
-    def body(w_ref, c_ref, r_ref, res_ref, cot_ref, gain_ref, one_ref, three_ref, keep_one_ref, keep_three_ref, mine_ref, pack_ref):
-        pack_ref[:TB] = cot_ref[...]
-        g = gain_ref[...]
-        hi = g.astype(BF16)
-        g = g - hi.astype(F32)
-        mid = g.astype(BF16)
-        low = (g - mid.astype(F32)).astype(BF16)
-        row = lax.broadcasted_iota(jnp.int32, (16, width), 0)
-        parts = jnp.where(row == 0, hi.astype(F32), jnp.where(row == 1, mid.astype(F32), jnp.where(row == 2, low.astype(F32), 0.0)))
-        pack_ref[TB:] = parts.astype(BF16)
+
+    def body(w_ref, c_ref, r_ref, res_ref, one_ref, three_ref, keep_one_ref, keep_three_ref, mine_ref):
         for i in range(toks // (STEP * TB)):
             acc = dot_t(w_ref[rows:], c_ref[pl.ds(i * STEP * TB, STEP * TB)])
             for b in range(STEP):
@@ -170,22 +160,46 @@
 
     part = lambda dtype: jax.ShapeDtypeStruct((toks // TB, half, TB), dtype)
     return pl.pallas_call(
-        body, in_specs=vmem(6), out_specs=vmem(6),
-        out_shape=(part(BF16), part(BF16), part(F32), part(F32), jax.ShapeDtypeStruct((toks // TB, rows, TB), F32), jax.ShapeDtypeStruct((TB + 16, width), BF16)),
+        body, in_specs=vmem(4), out_specs=vmem(5),
+        out_shape=(part(BF16), part(BF16), part(F32), part(F32), jax.ShapeDtypeStruct((toks // TB, rows, TB), F32)),
         compiler_params=params(20), cost_estimate=cost(3, rows, depth, toks), name="near_sum",
-    )(weights, ctx, other, residual, cot, gain)
-
-
-def add_halves(mine, top, low, dtype, name):
+    )(weights, ctx, other, residual)
+
+
+def add_direct(mine, top, low, cot, gain):
     half = top.shape[1]
+    width = cot.shape[1]
+
+    def body(mine_ref, top_ref, low_ref, cot_ref, gain_ref, o_ref, pack_ref):
+        pack_ref[:TB] = cot_ref[...]
+        g = gain_ref[...]
+        hi = g.astype(BF16)
+        g = g - hi.astype(F32)
+        mid = g.astype(BF16)
+        low = (g - mid.astype(F32)).astype(BF16)
+        row = lax.broadcasted_iota(jnp.int32, (16, width), 0)
+        parts = jnp.where(row == 0, hi.astype(F32), jnp.where(row == 1, mid.astype(F32), jnp.where(row == 2, low.astype(F32), 0.0)))
+        pack_ref[TB:] = parts.astype(BF16)
+        o_ref[:, :half] = mine_ref[:, :half] + top_ref[...].astype(F32)
+        o_ref[:, half:] = mine_ref[:, half:] + low_ref[...].astype(F32)
+
+    return pl.pallas_call(
+        body, in_specs=vmem(5), out_specs=vmem(2), out_shape=(jax.ShapeDtypeStruct(mine.shape, F32), jax.ShapeDtypeStruct((TB + 16, width), BF16)),
+        name="add_direct", compiler_params=params(8),
+        cost_estimate=pl.CostEstimate(flops=1 * mine.size, bytes_accessed=9 * mine.size, transcendentals=0),
+    )(mine, top, low, cot, gain)
+
+
+def add_last(mine, top, low):
+    half = top.shape[1]
 
     def body(mine_ref, top_ref, low_ref, o_ref):
-        o_ref[:, :half] = (mine_ref[:, :half] + top_ref[...].astype(F32)).astype(dtype)
-        o_ref[:, half:] = (mine_ref[:, half:] + low_ref[...].astype(F32)).astype(dtype)
-
-    return pl.pallas_call(
-        body, in_specs=vmem(3), out_specs=vmem(1)[0], out_shape=jax.ShapeDtypeStruct(mine.shape, dtype), name=name, compiler_params=params(8),
-        cost_estimate=pl.CostEstimate(flops=mine.size, bytes_accessed=9 * mine.size, transcendentals=0),
+        o_ref[:, :half] = (mine_ref[:, :half] + top_ref[...].astype(F32)).astype(BF16)
+        o_ref[:, half:] = (mine_ref[:, half:] + low_ref[...].astype(F32)).astype(BF16)
+
+    return pl.pallas_call(
+        body, in_specs=vmem(3), out_specs=vmem(1)[0], out_shape=jax.ShapeDtypeStruct(mine.shape, BF16), name="add_last", compiler_params=params(8),
+        cost_estimate=pl.CostEstimate(flops=20000 * mine.size, bytes_accessed=7 * mine.size, transcendentals=0),
     )(mine, top, low)
 
 
@@ -201,9 +215,69 @@
     )(keep_one, keep_three, from_one, from_three)
 
 
-def over_mp(x):
-    n = lax.axis_size("mp")
-    return jnp.sum(lax.all_to_all(jnp.broadcast_to(x, (n, *x.shape)), "mp", split_axis=0, concat_axis=0, tiled=True), axis=0)
+def small(body, name, n_in, out_shape, *args, flops=0):
+    n_out = len(out_shape) if isinstance(out_shape, tuple) else 1
+    moved = sum(a.size * a.dtype.itemsize for a in args)
+    return pl.pallas_call(
+        body, in_specs=vmem(n_in), out_specs=vmem(n_out) if isinstance(out_shape, tuple) else vmem(1)[0], out_shape=out_shape, name=name,
+        compiler_params=params(12), cost_estimate=pl.CostEstimate(flops=flops, bytes_accessed=moved, transcendentals=0),
+    )(*args)
+
+
+def scaled_cotangent(pack, gain):
+    width = pack.shape[1]
+
+    def body(pack_ref, g_ref, o_ref):
+        o_ref[...] = (pack_ref[:TB].astype(F32) * g_ref[...]).T
+
+    return small(body, "scaled_cotangent", 2, jax.ShapeDtypeStruct((width, TB), F32), pack, gain, flops=pack.size)
+
+
+def partial_sums(x, scaled, copies):
+    def body(x_ref, s_ref, o_ref):
+        v = x_ref[...].reshape(scaled.shape).astype(F32)
+        s = s_ref[...]
+        sums = [jnp.sum(a, axis=0, keepdims=True) for a in (v, v * v, s, s * v)]
+        block = jnp.concatenate([*sums, jnp.zeros((4, TB), F32)], axis=0)
+        for i in range(copies):
+            o_ref[i] = block
+
+    return small(body, "partial_sums", 2, jax.ShapeDtypeStruct((copies, 8, TB), F32), x, scaled, flops=6 * x.size)
+
+
+def statistics(sums):
+    def body(s_ref, o_ref):
+        total = s_ref[0]
+        for i in range(1, sums.shape[0]):
+            total += s_ref[i]
+        mean = total[0:1] / D
+        rstd = lax.rsqrt(total[1:2] / D - mean * mean + EPS)
+        first = total[2:3] / D
+        second = rstd * (total[3:4] / D - mean * first)
+        o_ref[...] = jnp.concatenate([mean, rstd, first, second, jnp.zeros((4, TB), F32)], axis=0)
+
+    return small(body, "statistics", 1, jax.ShapeDtypeStruct(sums.shape[1:], F32), sums)
+
+
+def gradient(x, scaled, stats):
+    def body(x_ref, s_ref, st_ref, o_ref):
+        v = x_ref[...].reshape(scaled.shape).astype(F32)
+        mean, rstd, first, second = (st_ref[i:i + 1] for i in range(4))
+        xhat = (v - mean) * rstd
+        o_ref[...] = (rstd * (s_ref[...] - first - xhat * second)).T.astype(BF16)
+
+    return small(body, "gradient", 3, jax.ShapeDtypeStruct((TB, scaled.shape[0]), BF16), x, scaled, stats, flops=60000 * x.size)
+
+
+def layer_norm(x, stats, gain, bias):
+    width = gain.shape[1]
+
+    def body(x_ref, st_ref, g_ref, b_ref, o_ref):
+        v = x_ref[...].reshape(width, TB).astype(F32)
+        xhat = (v - st_ref[0:1]) * st_ref[1:2]
+        o_ref[...] = (xhat.T * g_ref[...] + b_ref[...]).astype(BF16)
+
+    return small(body, "layer_norm", 4, jax.ShapeDtypeStruct((TB, width), BF16), x, stats, gain, bias, flops=4 * x.size)
 
 
 def local(context, out_weight, residual, gain, bias, cot):
@@ -214,39 +288,28 @@
 
     far_sent, ctx, near_weights, own_weights = far_product(m.reshape(1), weights, ctx)
     far_got = swap_core(far_sent)
-    near_got = swap_core(near_product(near_weights, ctx))
     far_top, far_low = far_sum(own_weights, ctx, far_got)
+    near_got = swap_core(near_product(near_weights, ctx, far_top))
     relay_one = swap_y(far_top, 1)
     relay_three = swap_y(far_low, 3)
-    one, three, keep_one, keep_three, mine, pack = near_sum(own_weights, ctx, near_got, residual[0].T, cot[0], gain)
+    one, three, keep_one, keep_three, mine = near_sum(own_weights, ctx, near_got, residual[0].T)
     direct_one = swap_y(one, 1)
     direct_three = swap_y(three, 3)
     on_one, on_three = relay_sum(keep_one, keep_three, relay_one, relay_three)
     sum_one = swap_y(on_one, 1)
     sum_three = swap_y(on_three, 3)
+    mine, pack = add_direct(mine, direct_one, direct_three, cot[0], gain)
     pack_next = along_section(pack, -1)
-    mine = add_halves(mine, direct_one, direct_three, F32, "add_direct")
-    section_out = add_halves(mine, sum_three, sum_one, BF16, "add_last")
+    section_out = add_last(mine, sum_three, sum_one)
     got = lax.all_to_all(section_out, "dp", split_axis=0, concat_axis=0, tiled=True)
-
+    got_next = along_section(got, 1)
     parts = pack_next[TB:TB + 3].astype(F32)
-    gain_next = parts[0:1] + parts[1:2] + parts[2:3]
-    scaled = pack_next[:TB].astype(F32) * gain_next
-    width = float(D)
-
-    got_next = along_section(got, 1)
-    x = got.reshape(-1, TB).T.astype(F32)
-    sums = jnp.stack([jnp.sum(x, -1), jnp.sum(x * x, -1), jnp.sum(scaled, -1), jnp.sum(scaled * x, -1)])
-    sums = over_mp(sums)
-    average = sums[0] / width
-    rstd = lax.rsqrt(sums[1] / width - average * average + EPS)
-    first = sums[2] / width
-    second = rstd * (sums[3] / width - average * first)
-    ar_next = along_section(jnp.stack([average, rstd]), 1)
-    xhat = (x - average[:, None]) * rstd[:, None]
-    grad = (rstd[:, None] * (scaled - first[:, None] - xhat * second[:, None])).astype(BF16)
-    xn = got_next.reshape(-1, TB).T.astype(F32)
-    out = ((xn - ar_next[0][:, None]) * ar_next[1][:, None] * gain + bias).astype(BF16)
+    scaled = scaled_cotangent(pack_next, parts[0:1] + parts[1:2] + parts[2:3])
+    sums = lax.all_to_all(partial_sums(got, scaled, lax.axis_size("mp")), "mp", split_axis=0, concat_axis=0, tiled=True)
+    stats = statistics(sums)
+    stats_next = along_section(stats, 1)
+    grad = gradient(got, scaled, stats)
+    out = layer_norm(got_next, stats_next, gain, bias)
     return out[None], grad[None]
 
 

time: 98.9 us -> 95.5 us (0.966)
  waiting for transfers between devices: 29.4 us -> 20.8 us
  starting transfers between devices: 57.6 us -> 63.5 us
  Pallas kernels: 6.6 us -> 9.71 us
  other arithmetic: 2.74 us -> 0.02 us
  local copies, waits for them, and re-layouts: 1.08 us -> 0.02 us
    ppermute x6, waiting for transfers between devices: 11.5 us -> 2.13 us  [swap_y(): return lax.ppermute(x, 'mp', [(i, i ^ 2 * pair) for i in range(n)])]
    ppermute x3, waiting for transfers between devices: 3.81 us -> 7.95 us  [along_section(): return lax.ppermute(x, 'section', [(i, (i + by) % n) for i in range(n)])]
    all_to_all x1, starting transfers between devices: 6.89 us -> 10.7 us  [local(): lax.all_to_all(partial_sums(got, scaled, lax.axis_size('mp')), 'mp', spli...]
    ppermute x6, starting transfers between devices: 17.4 us -> 21.2 us  [swap_y(): return lax.ppermute(x, 'mp', [(i, i ^ 2 * pair) for i in range(n)])]
    all_to_all x1, waiting for transfers between devices: 7.34 us -> 4.08 us  [local(): lax.all_to_all(section_out, 'dp', split_axis=0, concat_axis=0, tiled=True)]
    pallas_call x4 -> x9, Pallas kernels: 3.17 us -> 6.31 us  [the longest x5 3.15 us: small(): pl.pallas_call(body, in_specs=vmem(n_in), out_specs=vmem(n_out) if isinst...]
    broadcast_in_dim x2 -> x0, other arithmetic: 2.01 us -> none  [local(): return (out[None], grad[None])]
    ppermute x3, starting transfers between devices: 14.9 us -> 13 us  [along_section(): return lax.ppermute(x, 'section', [(i, (i + by) % n) for i in range(n)])]
  transfers between devices with their start and end apart: 13 -> 13, of which waited for: 6 -> 6; matrix products, arithmetic and copies ran while one was open for 1% -> 0% of each run, Pallas kernels for 3% -> 4%
where the time goes in v2:
time: 95.5 us; the launch traced here: 94.9 us
  starting transfers between devices  63.5 us (66%)
  waiting for transfers between devices  20.8 us (22%)
  Pallas kernels  9.71 us (10%)
    ppermute x6, starting transfers between devices, swap_y(): return lax.ppermute(x, 'mp', [(i, i ^ 2 * pair) for i in range(n)])  21.2 us
    ppermute x2, starting transfers between devices, swap_core(): return lax.ppermute(x, 'mp', [(i, i ^ 1) for i in range(n)])  14.7 us
    ppermute x3, starting transfers between devices, along_section(): return lax.ppermute(x, 'section', [(i, (i + by) % n) for i in range(n)])  13 us
    all_to_all x1, starting transfers between devices, local(): lax.all_to_all(partial_sums(got, scaled, lax.axis_size('mp')), 'mp', spli...  10.7 us
    ppermute x3, waiting for transfers between devices, along_section(): return lax.ppermute(x, 'section', [(i, (i + by) % n) for i in range(n)])  7.95 us
    all_to_all x1, waiting for transfers between devices, local(): lax.all_to_all(partial_sums(got, scaled, lax.axis_size('mp')), 'mp', spli...  5.29 us
    all_to_all x1, waiting for transfers between devices, local(): lax.all_to_all(section_out, 'dp', split_axis=0, concat_axis=0, tiled=True)  4.08 us
    all_to_all x1, starting transfers between devices, local(): lax.all_to_all(section_out, 'dp', split_axis=0, concat_axis=0, tiled=True)  3.99 us
  transfers between devices with their start and end apart: 13, of which 6 were waited for; matrix products, arithmetic and copies ran while one was open for 0% of the time, Pallas kernels for 4%

profile of v2, /device:TPU:1, one launch (start us, length us, event | category | flops | bytes accessed | tf_op | source)
XLA Modules:
  0.0 94.9 jit_solution(5365091692236417919)
XLA Ops:
  0.6 2.7 %far_product.1 = (bf16[8,192,128]{2,1,0:T(8,128)(2,1)S(1)}, bf16[1024,768]{1,0:T(8,128)(2,1)S(1)}, bf16[576,768]{1,0:T(8,128)(2,1)S(1)}, bf16[768,768]{1,0:T(8,128)(2,1)S(1)}) custom-call(s32[1]{0:T(128)} %bitcast.me_ref, bf16[8,192,768]{2,1,0:T(8,128)(2,1)} %bitcast.13, bf16[1024,768]{1,0:T(8,128)(2,1)} %bitcast.14), custom_call_target="tpu_custom_call" | custom-call | flops 301989888 | bytes 2654208 | tf_op jit(solution)/shard_map/far_product/pallas_call | solution.py:90
  3.3 12.4 %collective-permute-start = (bf16[8,192,128]{2,1,0:T(8,128)(2,1)S(1)}, bf16[8,192,128]{2,1,0:T(8,128)(2,1)S(1)}, u32[]{:S(2)}, u32[]{:S(2)}) collective-permute-start(bf16[8,192,128]{2,1,0:T(8,128)(2,1)S(1)} %get-tuple-element.20), channel_id=1, source_target_pairs={{0,8},{8,0},{16,24},{24,16},{32,40},{40,32},{48,56},{56,48},{1,9},... | collective-permute-start | bytes 1179656 | tf_op jit(solution)/shard_map/ppermute | solution.py:19
  15.7 1.3 %collective-permute-done.r_ref = bf16[8,192,128]{2,1,0:T(8,128)(2,1)S(1)} collective-permute-done((bf16[8,192,128]{2,1,0:T(8,128)(2,1)S(1)}, bf16[8,192,128]{2,1,0:T(8,128)(2,1)S(1)}, u32[]{:S(2)}, u32[]{:S(2)}) %collective-permute-start) | collective-permute-done | bytes 393248 | tf_op jit(solution)/shard_map/ppermute | solution.py:19
  17.1 0.7 far_sum.1
  17.7 0.0 copy-start
  17.8 1.1 %near_product.1 = bf16[3,8,192,128]{3,2,1,0:T(8,128)(2,1)S(1)} custom-call(bf16[576,768]{1,0:T(8,128)(2,1)S(1)} %get-tuple-element.19.w_ref, bf16[1024,768]{1,0:T(8,128)(2,1)S(1)} %get-tuple-element.18.c_ref, bf16[8,96,128]{2,1,0:T(8,128)(2,1)S(1)} %get-tuple-element.21.after_ref), custom_call_target="tpu_custom_call" | custom-call | flops 905969664 | bytes 4816896 | tf_op jit(solution)/shard_map/near_product/pallas_call | solution.py:116
  18.9 2.3 %collective-permute-start.1 = (bf16[3,8,192,128]{3,2,1,0:T(8,128)(2,1)S(1)}, bf16[3,8,192,128]{3,2,1,0:T(8,128)(2,1)S(1)}, u32[]{:S(2)}, u32[]{:S(2)}) collective-permute-start(bf16[3,8,192,128]{3,2,1,0:T(8,128)(2,1)S(1)} %near_product.1), channel_id=1, source_target_pairs={{0,8},{8,0},{16,24},{24,16},{32,40},{40,32},{48,56},{56,48},{1,9},... | collective-permute-start | bytes 3538952 | tf_op jit(solution)/shard_map/ppermute | solution.py:19
  21.2 1.9 %collective-permute-start.5 = (bf16[8,96,128]{2,1,0:T(8,128)(2,1)S(1)}, bf16[8,96,128]{2,1,0:T(8,128)(2,1)S(1)}, u32[]{:S(2)}, u32[]{:S(2)}) collective-permute-start(bf16[8,96,128]{2,1,0:T(8,128)(2,1)S(1)} %get-tuple-element.28), channel_id=1, source_target_pairs={{0,48},{8,56},{16,32},{24,40},{32,16},{40,24},{48,0},{56,8},{1,49}... | collective-permute-start | bytes 589832 | tf_op jit(solution)/shard_map/ppermute | solution.py:24
  23.1 1.9 %collective-permute-start.4 = (bf16[8,96,128]{2,1,0:T(8,128)(2,1)S(1)}, bf16[8,96,128]{2,1,0:T(8,128)(2,1)S(1)}, u32[]{:S(2)}, u32[]{:S(2)}) collective-permute-start(bf16[8,96,128]{2,1,0:T(8,128)(2,1)S(1)} %get-tuple-element.21.after_ref), channel_id=1, source_target_pairs={{0,16},{8,24},{16,0},{24,8},{32,48},{40,56},{48,32},{56,40},{1,17}... | collective-permute-start | bytes 589832 | tf_op jit(solution)/shard_map/ppermute | solution.py:24
  25.0 0.0 collective-permute-done.1.r_ref
  25.0 0.0 copy-done
  25.0 0.0 copy-start.1
  25.0 0.0 copy-start.2
  25.1 1.1 %near_sum.1 = (bf16[8,96,128]{2,1,0:T(8,128)(2,1)S(1)}, bf16[8,96,128]{2,1,0:T(8,128)(2,1)S(1)}, f32[8,96,128]{2,1,0:T(8,128)S(1)}, f32[8,96,128]{2,1,0:T(8,128)S(1)}, f32[8,192,128]{2,1,0:T(8,128)S(1)}) custom-call(bf16[768,768]{1,0:T(8,128)(2,1)S(1)} %get-tuple-element.17.w_ref, bf16[1024,768]{1,0:T(8,128)(2,1)S(1)} %get-tuple-element.18.c_ref, ...), custom_call_target="tpu_custom_call" | custom-call | flops 905969664 | bytes 4816896 | tf_op jit(solution)/shard_map/near_sum/pallas_call | solution.py:162
  26.2 4.3 %collective-permute-start.2 = (bf16[8,96,128]{2,1,0:T(8,128)(2,1)S(1)}, bf16[8,96,128]{2,1,0:T(8,128)(2,1)S(1)}, u32[]{:S(2)}, u32[]{:S(2)}) collective-permute-start(bf16[8,96,128]{2,1,0:T(8,128)(2,1)S(1)} %get-tuple-element.23), channel_id=1, source_target_pairs={{0,16},{8,24},{16,0},{24,8},{32,48},{40,56},{48,32},{56,40},{1,17}... | collective-permute-start | bytes 589832 | tf_op jit(solution)/shard_map/ppermute | solution.py:24
  30.4 5.5 %collective-permute-start.3 = (bf16[8,96,128]{2,1,0:T(8,128)(2,1)S(1)}, bf16[8,96,128]{2,1,0:T(8,128)(2,1)S(1)}, u32[]{:S(2)}, u32[]{:S(2)}) collective-permute-start(bf16[8,96,128]{2,1,0:T(8,128)(2,1)S(1)} %get-tuple-element.24), channel_id=1, source_target_pairs={{0,48},{8,56},{16,32},{24,40},{32,16},{40,24},{48,0},{56,8},{1,49}... | collective-permute-start | bytes 589832 | tf_op jit(solution)/shard_map/ppermute | solution.py:24
  35.9 0.0 collective-permute-done.5.from_three_ref
  35.9 2.1 %collective-permute-done.4.from_one_ref = bf16[8,96,128]{2,1,0:T(8,128)(2,1)S(1)} collective-permute-done((bf16[8,96,128]{2,1,0:T(8,128)(2,1)S(1)}, bf16[8,96,128]{2,1,0:T(8,128)(2,1)S(1)}, u32[]{:S(2)}, u32[]{:S(2)}) %collective-permute-start.4) | collective-permute-done | bytes 196640 | tf_op jit(solution)/shard_map/ppermute | solution.py:24
  38.1 0.1 relay_sum.1
  38.1 5.7 %collective-permute-start.6 = (bf16[8,96,128]{2,1,0:T(8,128)(2,1)S(1)}, bf16[8,96,128]{2,1,0:T(8,128)(2,1)S(1)}, u32[]{:S(2)}, u32[]{:S(2)}) collective-permute-start(bf16[8,96,128]{2,1,0:T(8,128)(2,1)S(1)} %get-tuple-element.29), channel_id=1, source_target_pairs={{0,48},{8,56},{16,32},{24,40},{32,16},{40,24},{48,0},{56,8},{1,49}... | collective-permute-start | bytes 589832 | tf_op jit(solution)/shard_map/ppermute | solution.py:24
  43.8 1.9 %collective-permute-start.7 = (bf16[8,96,128]{2,1,0:T(8,128)(2,1)S(1)}, bf16[8,96,128]{2,1,0:T(8,128)(2,1)S(1)}, u32[]{:S(2)}, u32[]{:S(2)}) collective-permute-start(bf16[8,96,128]{2,1,0:T(8,128)(2,1)S(1)} %get-tuple-element.30), channel_id=1, source_target_pairs={{0,16},{8,24},{16,0},{24,8},{32,48},{40,56},{48,32},{56,40},{1,17}... | collective-permute-start | bytes 589832 | tf_op jit(solution)/shard_map/ppermute | solution.py:24
  45.7 0.0 collective-permute-done.2.top_ref
  45.7 0.0 collective-permute-done.3.low_ref
  45.7 0.0 copy-done.1
  45.8 0.0 copy-done.2
  45.8 0.1 add_direct.1
  45.9 9.2 %collective-permute-start.9 = (bf16[144,1536]{1,0:T(8,128)(2,1)S(1)}, bf16[144,1536]{1,0:T(8,128)(2,1)S(1)}, u32[]{:S(2)}, u32[]{:S(2)}) collective-permute-start(bf16[144,1536]{1,0:T(8,128)(2,1)S(1)} %get-tuple-element.31), channel_id=1, source_target_pairs={{0,704},{64,0},{128,64},{192,128},{256,192},{320,256},{384,320},{4... | collective-permute-start | bytes 1327112 | tf_op jit(solution)/shard_map/ppermute | solution.py:29
  55.1 0.0 collective-permute-done.6.top_ref
  55.1 0.0 collective-permute-done.7.low_ref
  55.1 0.8 add_last.1
  55.9 4.0 %all-to-all-start = ((bf16[8,192,128]{2,1,0:T(8,128)(2,1)}), bf16[8,192,128]{2,1,0:T(8,128)(2,1)S(1)}, u32[]{:S(2)}, u32[]{:S(2)}) async-start(bf16[8,192,128]{2,1,0:T(8,128)(2,1)} %add_last.1), calls=%async_computation | async-start | bytes 786432 | tf_op jit(solution)/shard_map/all_to_all | solution.py:304
  59.9 2.5 %collective-permute-done.9.pack_ref = bf16[144,1536]{1,0:T(8,128)(2,1)S(1)} collective-permute-done((bf16[144,1536]{1,0:T(8,128)(2,1)S(1)}, bf16[144,1536]{1,0:T(8,128)(2,1)S(1)}, u32[]{:S(2)}, u32[]{:S(2)}) %collective-permute-start.9) | collective-permute-done | bytes 442400 | tf_op jit(solution)/shard_map/ppermute | solution.py:29
  62.4 0.3 scaled_cotangent.1.s_ref
  62.6 4.1 %all-to-all-done.x_ref = bf16[8,192,128]{2,1,0:T(8,128)(2,1)S(1)} async-done(((bf16[8,192,128]{2,1,0:T(8,128)(2,1)}), bf16[8,192,128]{2,1,0:T(8,128)(2,1)S(1)}, u32[]{:S(2)}, u32[]{:S(2)}) %all-to-all-start) | async-done | bytes 393248 | tf_op jit(solution)/shard_map/all_to_all | solution.py:304
  66.7 0.8 partial_sums.1
  67.6 10.7 %all-to-all-start.1 = ((f32[8,8,128]{2,1,0:T(8,128)}), f32[8,8,128]{2,1,0:T(8,128)S(1)}, u32[]{:S(2)}, u32[]{:S(2)}) async-start(f32[8,8,128]{2,1,0:T(8,128)} %partial_sums.1), calls=%async_computation.1 | async-start | bytes 65536 | tf_op jit(solution)/shard_map/all_to_all | solution.py:308
  78.2 1.9 %collective-permute-start.8 = (bf16[8,192,128]{2,1,0:T(8,128)(2,1)S(1)}, bf16[8,192,128]{2,1,0:T(8,128)(2,1)S(1)}, u32[]{:S(2)}, u32[]{:S(2)}) collective-permute-start(bf16[8,192,128]{2,1,0:T(8,128)(2,1)S(1)} %all-to-all-done.x_ref), channel_id=1, source_target_pairs={{0,64},{64,128},{128,192},{192,256},{256,320},{320,384},{384,448},... | collective-permute-start | bytes 1179656 | tf_op jit(solution)/shard_map/ppermute | solution.py:29
  80.1 5.3 %all-to-all-done.1.s_ref = f32[8,8,128]{2,1,0:T(8,128)S(1)} async-done(((f32[8,8,128]{2,1,0:T(8,128)}), f32[8,8,128]{2,1,0:T(8,128)S(1)}, u32[]{:S(2)}, u32[]{:S(2)}) %all-to-all-start.1) | async-done | bytes 32800 | tf_op jit(solution)/shard_map/all_to_all | solution.py:308
  85.4 0.0 copy-start.3
  85.5 1.9 %collective-permute-start.10 = (f32[8,128]{1,0:T(8,128)S(1)}, f32[8,128]{1,0:T(8,128)S(1)}, u32[]{:S(2)}, u32[]{:S(2)}) collective-permute-start(f32[8,128]{1,0:T(8,128)S(1)} %statistics.1.st_ref), channel_id=1, source_target_pairs={{0,64},{64,128},{128,192},{192,256},{256,320},{320,384},{384,448},... | collective-permute-start | bytes 12296 | tf_op jit(solution)/shard_map/ppermute | solution.py:29
  87.4 1.0 %gradient.1 = bf16[128,1536]{1,0:T(8,128)(2,1)} custom-call(bf16[8,192,128]{2,1,0:T(8,128)(2,1)S(1)} %all-to-all-done.x_ref, f32[1536,128]{1,0:T(8,128)S(1)} %scaled_cotangent.1.s_ref, f32[8,128]{1,0:T(8,128)S(1)} %statistics.1.st_ref), custom_call_target="tpu_custom_call" | custom-call | flops 11796480000 | bytes 1183744 | tf_op jit(solution)/shard_map/gradient/pallas_call | solution.py:221
  88.4 5.5 %collective-permute-done.10.st_ref = f32[8,128]{1,0:T(8,128)S(1)} collective-permute-done((f32[8,128]{1,0:T(8,128)S(1)}, f32[8,128]{1,0:T(8,128)S(1)}, u32[]{:S(2)}, u32[]{:S(2)}) %collective-permute-start.10) | collective-permute-done | bytes 4128 | tf_op jit(solution)/shard_map/ppermute | solution.py:29
  93.9 0.0 collective-permute-done.8.x_ref
  93.9 0.0 copy-done.3
  93.9 1.0 %layer_norm.1 = bf16[128,1536]{1,0:T(8,128)(2,1)} custom-call(bf16[8,192,128]{2,1,0:T(8,128)(2,1)S(1)} %collective-permute-done.8.x_ref, f32[8,128]{1,0:T(8,128)S(1)} %collective-permute-done.10.st_ref, f32[1,1536]{1,0:T(1,128)S(1)} %copy-done.2, f32[1,1536]{1,0:T(1,128)S(1)} %copy-done.3), custom_call_target="tpu_custom_call" | custom-call | flops 786432 | bytes 409600 | tf_op jit(solution)/shard_map/layer_norm/pallas_call | solution.py:221
  (3 shorter events, 0.0 us)
Async XLA Ops:
  3.3 13.8 %collective-permute-start = (bf16[8,192,128]{2,1,0:T(8,128)(2,1)S(1)}, bf16[8,192,128]{2,1,0:T(8,128)(2,1)S(1)}, u32[]{:S(2)}, u32[]{:S(2)}) collective-permute-start(bf16[8,192,128]{2,1,0:T(8,128)(2,1)S(1)} %get-tuple-element.20), channel_id=1, source_target_pairs={{0,8},{8,0},{16,24},{24,16},{32,40},{40,32},{48,56},{56,48},{1,9},... | collective-permute-start | bytes 1179656 | tf_op jit(solution)/shard_map/ppermute | solution.py:19
  17.7 7.3 %copy-start = (bf16[1,1024,192]{1,2,0:T(8,128)(2,1)S(1)}, bf16[1,1024,192]{1,2,0:T(8,128)(2,1)}, u32[]{:S(2)}) copy-start(bf16[1,1024,192]{1,2,0:T(8,128)(2,1)} %param.8) | copy-start | bytes 1179652
  18.9 6.1 %collective-permute-start.1 = (bf16[3,8,192,128]{3,2,1,0:T(8,128)(2,1)S(1)}, bf16[3,8,192,128]{3,2,1,0:T(8,128)(2,1)S(1)}, u32[]{:S(2)}, u32[]{:S(2)}) collective-permute-start(bf16[3,8,192,128]{3,2,1,0:T(8,128)(2,1)S(1)} %near_product.1), channel_id=1, source_target_pairs={{0,8},{8,0},{16,24},{24,16},{32,40},{40,32},{48,56},{56,48},{1,9},... | collective-permute-start | bytes 3538952 | tf_op jit(solution)/shard_map/ppermute | solution.py:19
  21.2 14.8 %collective-permute-start.5 = (bf16[8,96,128]{2,1,0:T(8,128)(2,1)S(1)}, bf16[8,96,128]{2,1,0:T(8,128)(2,1)S(1)}, u32[]{:S(2)}, u32[]{:S(2)}) collective-permute-start(bf16[8,96,128]{2,1,0:T(8,128)(2,1)S(1)} %get-tuple-element.28), channel_id=1, source_target_pairs={{0,48},{8,56},{16,32},{24,40},{32,16},{40,24},{48,0},{56,8},{1,49}... | collective-permute-start | bytes 589832 | tf_op jit(solution)/shard_map/ppermute | solution.py:24
  23.1 15.0 %collective-permute-start.4 = (bf16[8,96,128]{2,1,0:T(8,128)(2,1)S(1)}, bf16[8,96,128]{2,1,0:T(8,128)(2,1)S(1)}, u32[]{:S(2)}, u32[]{:S(2)}) collective-permute-start(bf16[8,96,128]{2,1,0:T(8,128)(2,1)S(1)} %get-tuple-element.21.after_ref), channel_id=1, source_target_pairs={{0,16},{8,24},{16,0},{24,8},{32,48},{40,56},{48,32},{56,40},{1,17}... | collective-permute-start | bytes 589832 | tf_op jit(solution)/shard_map/ppermute | solution.py:24
  25.0 20.7 %copy-start.1 = (bf16[1,128,1536]{2,1,0:T(8,128)(2,1)S(1)}, bf16[1,128,1536]{2,1,0:T(8,128)(2,1)}, u32[]{:S(2)}) copy-start(bf16[1,128,1536]{2,1,0:T(8,128)(2,1)} %param.11) | copy-start | bytes 1179652
  25.0 20.7 %copy-start.2 = (f32[1,1536]{1,0:T(1,128)S(1)}, f32[1,1536]{1,0:T(1,128)}, u32[]{:S(2)}) copy-start(f32[1,1536]{1,0:T(1,128)} %g_ref.1) | copy-start | bytes 18436
  26.2 19.5 %collective-permute-start.2 = (bf16[8,96,128]{2,1,0:T(8,128)(2,1)S(1)}, bf16[8,96,128]{2,1,0:T(8,128)(2,1)S(1)}, u32[]{:S(2)}, u32[]{:S(2)}) collective-permute-start(bf16[8,96,128]{2,1,0:T(8,128)(2,1)S(1)} %get-tuple-element.23), channel_id=1, source_target_pairs={{0,16},{8,24},{16,0},{24,8},{32,48},{40,56},{48,32},{56,40},{1,17}... | collective-permute-start | bytes 589832 | tf_op jit(solution)/shard_map/ppermute | solution.py:24
  30.4 15.3 %collective-permute-start.3 = (bf16[8,96,128]{2,1,0:T(8,128)(2,1)S(1)}, bf16[8,96,128]{2,1,0:T(8,128)(2,1)S(1)}, u32[]{:S(2)}, u32[]{:S(2)}) collective-permute-start(bf16[8,96,128]{2,1,0:T(8,128)(2,1)S(1)} %get-tuple-element.24), channel_id=1, source_target_pairs={{0,48},{8,56},{16,32},{24,40},{32,16},{40,24},{48,0},{56,8},{1,49}... | collective-permute-start | bytes 589832 | tf_op jit(solution)/shard_map/ppermute | solution.py:24
  38.1 16.9 %collective-permute-start.6 = (bf16[8,96,128]{2,1,0:T(8,128)(2,1)S(1)}, bf16[8,96,128]{2,1,0:T(8,128)(2,1)S(1)}, u32[]{:S(2)}, u32[]{:S(2)}) collective-permute-start(bf16[8,96,128]{2,1,0:T(8,128)(2,1)S(1)} %get-tuple-element.29), channel_id=1, source_target_pairs={{0,48},{8,56},{16,32},{24,40},{32,16},{40,24},{48,0},{56,8},{1,49}... | collective-permute-start | bytes 589832 | tf_op jit(solution)/shard_map/ppermute | solution.py:24
  43.8 11.3 %collective-permute-start.7 = (bf16[8,96,128]{2,1,0:T(8,128)(2,1)S(1)}, bf16[8,96,128]{2,1,0:T(8,128)(2,1)S(1)}, u32[]{:S(2)}, u32[]{:S(2)}) collective-permute-start(bf16[8,96,128]{2,1,0:T(8,128)(2,1)S(1)} %get-tuple-element.30), channel_id=1, source_target_pairs={{0,16},{8,24},{16,0},{24,8},{32,48},{40,56},{48,32},{56,40},{1,17}... | collective-permute-start | bytes 589832 | tf_op jit(solution)/shard_map/ppermute | solution.py:24
  45.9 16.5 %collective-permute-start.9 = (bf16[144,1536]{1,0:T(8,128)(2,1)S(1)}, bf16[144,1536]{1,0:T(8,128)(2,1)S(1)}, u32[]{:S(2)}, u32[]{:S(2)}) collective-permute-start(bf16[144,1536]{1,0:T(8,128)(2,1)S(1)} %get-tuple-element.31), channel_id=1, source_target_pairs={{0,704},{64,0},{128,64},{192,128},{256,192},{320,256},{384,320},{4... | collective-permute-start | bytes 1327112 | tf_op jit(solution)/shard_map/ppermute | solution.py:29
  55.9 10.8 %all-to-all-start = ((bf16[8,192,128]{2,1,0:T(8,128)(2,1)}), bf16[8,192,128]{2,1,0:T(8,128)(2,1)S(1)}, u32[]{:S(2)}, u32[]{:S(2)}) async-start(bf16[8,192,128]{2,1,0:T(8,128)(2,1)} %add_last.1), calls=%async_computation | async-start | bytes 786432 | tf_op jit(solution)/shard_map/all_to_all | solution.py:304
  67.6 17.9 %all-to-all-start.1 = ((f32[8,8,128]{2,1,0:T(8,128)}), f32[8,8,128]{2,1,0:T(8,128)S(1)}, u32[]{:S(2)}, u32[]{:S(2)}) async-start(f32[8,8,128]{2,1,0:T(8,128)} %partial_sums.1), calls=%async_computation.1 | async-start | bytes 65536 | tf_op jit(solution)/shard_map/all_to_all | solution.py:308
  78.2 15.7 %collective-permute-start.8 = (bf16[8,192,128]{2,1,0:T(8,128)(2,1)S(1)}, bf16[8,192,128]{2,1,0:T(8,128)(2,1)S(1)}, u32[]{:S(2)}, u32[]{:S(2)}) collective-permute-start(bf16[8,192,128]{2,1,0:T(8,128)(2,1)S(1)} %all-to-all-done.x_ref), channel_id=1, source_target_pairs={{0,64},{64,128},{128,192},{192,256},{256,320},{320,384},{384,448},... | collective-permute-start | bytes 1179656 | tf_op jit(solution)/shard_map/ppermute | solution.py:29
  85.4 8.4 %copy-start.3 = (f32[1,1536]{1,0:T(1,128)S(1)}, f32[1,1536]{1,0:T(1,128)}, u32[]{:S(2)}) copy-start(f32[1,1536]{1,0:T(1,128)} %b_ref.1) | copy-start | bytes 18436
  85.5 8.4 %collective-permute-start.10 = (f32[8,128]{1,0:T(8,128)S(1)}, f32[8,128]{1,0:T(8,128)S(1)}, u32[]{:S(2)}, u32[]{:S(2)}) collective-permute-start(f32[8,128]{1,0:T(8,128)S(1)} %statistics.1.st_ref), channel_id=1, source_target_pairs={{0,64},{64,128},{128,192},{192,256},{256,320},{320,384},{384,448},... | collective-permute-start | bytes 12296 | tf_op jit(solution)/shard_map/ppermute | solution.py:29

commit v3 on v2

--- a/solution.py
+++ b/solution.py
@@ -45,60 +45,72 @@
     return pl.CostEstimate(flops=2 * n * rows * depth * toks, bytes_accessed=2 * n * rows * (depth + 2 * toks) + 2 * toks * depth, transcendentals=0)
 
 
+def block_of(me, order, core):
+    return (((me >> 1) ^ order) << 1) + core
+
+
 def far_product(me, weights, ctx):
-    n_blocks, rows, depth = weights.shape
+    rows, depth = weights.shape[1:]
     toks = ctx.shape[0]
     n_parts = 4
 
-    def body(me_ref, w_ref, c_ref, far_ref, ctx_ref, near_w_ref, own_w_ref, far_w, c_sem, w_sem, own_sem):
+    def body(me_ref, w_ref, c_ref, far_ref, ctx_ref, far_w, c_sem, w_sem):
         me = me_ref[0]
-        core = me & 1
-
-        def block(k, c):
-            return (((me >> 1) ^ ORDER[k]) << 1) + c
 
         def c_copy(i):
             part = pl.ds(i * (toks // n_parts), toks // n_parts)
             return pltpu.make_async_copy(c_ref.at[part], ctx_ref.at[part], c_sem.at[i])
 
-        def w_copy(k):
-            to = far_w if k == 0 else near_w_ref.at[pl.ds((k - 1) * rows, rows)]
-            return pltpu.make_async_copy(w_ref.at[block(k, 1 - core)], to, w_sem.at[k])
-
-        def own_copy(k):
-            return pltpu.make_async_copy(w_ref.at[block(k, core)], own_w_ref.at[pl.ds(k * rows, rows)], own_sem.at[k])
-
-        w_copy(0).start()
+        w_copy = pltpu.make_async_copy(w_ref.at[block_of(me, ORDER[0], 1 - (me & 1))], far_w, w_sem)
+        w_copy.start()
         for i in range(n_parts):
             c_copy(i).start()
-        for k in range(1, 4):
-            w_copy(k).start()
-        for k in range(4):
-            own_copy(k).start()
-        w_copy(0).wait()
+        w_copy.wait()
         for i in range(n_parts):
             c_copy(i).wait()
         for i in range(toks // (STEP * TB)):
             acc = dot_t(far_w[...], ctx_ref[pl.ds(i * STEP * TB, STEP * TB)])
             for b in range(STEP):
                 far_ref[STEP * i + b] = acc[:, b * TB:(b + 1) * TB].astype(BF16)
-        for k in range(1, 4):
-            w_copy(k).wait()
-        for k in range(4):
-            own_copy(k).wait()
 
     return pl.pallas_call(
         body,
         in_specs=[pl.BlockSpec(memory_space=pltpu.SMEM), pl.BlockSpec(memory_space=pltpu.HBM), pl.BlockSpec(memory_space=pltpu.HBM)],
-        out_specs=vmem(4),
-        out_shape=(
-            jax.ShapeDtypeStruct((toks // TB, rows, TB), BF16),
-            jax.ShapeDtypeStruct((toks, depth), BF16),
-            jax.ShapeDtypeStruct((3 * rows, depth), BF16),
-            jax.ShapeDtypeStruct((4 * rows, depth), BF16),
-        ),
-        scratch_shapes=[pltpu.VMEM((rows, depth), BF16), pltpu.SemaphoreType.DMA((n_parts,)), pltpu.SemaphoreType.DMA((4,)), pltpu.SemaphoreType.DMA((4,))],
+        out_specs=vmem(2),
+        out_shape=(jax.ShapeDtypeStruct((toks // TB, rows, TB), BF16), jax.ShapeDtypeStruct((toks, depth), BF16)),
+        scratch_shapes=[pltpu.VMEM((rows, depth), BF16), pltpu.SemaphoreType.DMA((n_parts,)), pltpu.SemaphoreType.DMA],
         compiler_params=params(16), cost_estimate=cost(1, rows, depth, toks), name="far_product",
+    )(me, weights, ctx)
+
+
+def own_far_product(me, weights, ctx):
+    rows, depth = weights.shape[1:]
+    toks = ctx.shape[0]
+
+    def body(me_ref, w_ref, c_ref, far_ref, near_w_ref, own_w_ref, far_w, far_sem, near_sem, own_sem):
+        me = me_ref[0]
+        core = me & 1
+        far_copy = pltpu.make_async_copy(w_ref.at[block_of(me, ORDER[0], core)], far_w, far_sem)
+        copies = [pltpu.make_async_copy(w_ref.at[block_of(me, ORDER[k], 1 - core)], near_w_ref.at[pl.ds((k - 1) * rows, rows)], near_sem.at[k - 1]) for k in range(1, 4)]
+        copies += [pltpu.make_async_copy(w_ref.at[block_of(me, ORDER[k], core)], own_w_ref.at[pl.ds((k - 1) * rows, rows)], own_sem.at[k - 1]) for k in range(1, 4)]
+        far_copy.start()
+        for copy in copies:
+            copy.start()
+        far_copy.wait()
+        for i in range(toks // (STEP * TB)):
+            acc = dot_t(far_w[...], c_ref[pl.ds(i * STEP * TB, STEP * TB)])
+            for b in range(STEP):
+                far_ref[STEP * i + b] = acc[:, b * TB:(b + 1) * TB]
+        for copy in copies:
+            copy.wait()
+
+    return pl.pallas_call(
+        body,
+        in_specs=[pl.BlockSpec(memory_space=pltpu.SMEM), pl.BlockSpec(memory_space=pltpu.HBM), *vmem(1)],
+        out_specs=vmem(3),
+        out_shape=(jax.ShapeDtypeStruct((toks // TB, rows, TB), F32), jax.ShapeDtypeStruct((3 * rows, depth), BF16), jax.ShapeDtypeStruct((3 * rows, depth), BF16)),
+        scratch_shapes=[pltpu.VMEM((rows, depth), BF16), pltpu.SemaphoreType.DMA, pltpu.SemaphoreType.DMA((3,)), pltpu.SemaphoreType.DMA((3,))],
+        compiler_params=params(16), cost_estimate=cost(2, rows, depth, toks), name="own_far_product",
     )(me, weights, ctx)
 
 
@@ -119,34 +131,28 @@
     )(weights, ctx, after)
 
 
-def far_sum(weights, ctx, other):
-    toks, depth = ctx.shape
-    rows = weights.shape[0] // 4
-    half = rows // 2
-
-    def body(w_ref, c_ref, r_ref, top_ref, low_ref):
-        for i in range(toks // (STEP * TB)):
-            acc = dot_t(w_ref[:rows], c_ref[pl.ds(i * STEP * TB, STEP * TB)])
-            for b in range(STEP):
-                total = (acc[:, b * TB:(b + 1) * TB] + r_ref[STEP * i + b].astype(F32)).astype(BF16)
-                top_ref[STEP * i + b] = total[:half]
-                low_ref[STEP * i + b] = total[half:]
-
-    shape = jax.ShapeDtypeStruct((toks // TB, half, TB), BF16)
-    return pl.pallas_call(
-        body, in_specs=vmem(3), out_specs=vmem(2), out_shape=(shape, shape),
-        compiler_params=params(16), cost_estimate=cost(1, rows, depth, toks), name="far_sum",
-    )(weights, ctx, other)
+def far_sum(own, other):
+    half = own.shape[1] // 2
+
+    def body(own_ref, other_ref, top_ref, low_ref):
+        top_ref[...] = (own_ref[:, :half] + other_ref[:, :half].astype(F32)).astype(BF16)
+        low_ref[...] = (own_ref[:, half:] + other_ref[:, half:].astype(F32)).astype(BF16)
+
+    shape = jax.ShapeDtypeStruct((own.shape[0], half, own.shape[2]), BF16)
+    return pl.pallas_call(
+        body, in_specs=vmem(2), out_specs=vmem(2), out_shape=(shape, shape), name="far_sum", compiler_params=params(8),
+        cost_estimate=pl.CostEstimate(flops=own.size, bytes_accessed=8 * own.size, transcendentals=0),
+    )(own, other)
 
 
 def near_sum(weights, ctx, other, residual):
     toks, depth = ctx.shape
-    rows = weights.shape[0] // 4
+    rows = weights.shape[0] // 3
     half = rows // 2
 
     def body(w_ref, c_ref, r_ref, res_ref, one_ref, three_ref, keep_one_ref, keep_three_ref, mine_ref):
         for i in range(toks // (STEP * TB)):
-            acc = dot_t(w_ref[rows:], c_ref[pl.ds(i * STEP * TB, STEP * TB)])
+            acc = dot_t(w_ref[...], c_ref[pl.ds(i * STEP * TB, STEP * TB)])
             for b in range(STEP):
                 t = STEP * i + b
                 cut = slice(b * TB, (b + 1) * TB)
@@ -235,9 +241,13 @@
 
 def partial_sums(x, scaled, copies):
     def body(x_ref, s_ref, o_ref):
-        v = x_ref[...].reshape(scaled.shape).astype(F32)
-        s = s_ref[...]
-        sums = [jnp.sum(a, axis=0, keepdims=True) for a in (v, v * v, s, s * v)]
+        groups, rows = x.shape[:2]
+        totals = [jnp.zeros((rows, TB), F32)] * 4
+        for i in range(groups):
+            v = x_ref[i].astype(F32)
+            s = s_ref[i * rows:(i + 1) * rows]
+            totals = [t + a for t, a in zip(totals, (v, v * v, s, s * v))]
+        sums = [jnp.sum(t, axis=0, keepdims=True) for t in totals]
         block = jnp.concatenate([*sums, jnp.zeros((4, TB), F32)], axis=0)
         for i in range(copies):
             o_ref[i] = block
@@ -286,9 +296,10 @@
     weights = pltpu.with_memory_space_constraint(weights, pltpu.HBM)
     ctx = pltpu.with_memory_space_constraint(context[0], pltpu.HBM)
 
-    far_sent, ctx, near_weights, own_weights = far_product(m.reshape(1), weights, ctx)
+    far_sent, ctx = far_product(m.reshape(1), weights, ctx)
     far_got = swap_core(far_sent)
-    far_top, far_low = far_sum(own_weights, ctx, far_got)
+    far_own, near_weights, own_weights = own_far_product(m.reshape(1), weights, ctx)
+    far_top, far_low = far_sum(far_own, far_got)
     near_got = swap_core(near_product(near_weights, ctx, far_top))
     relay_one = swap_y(far_top, 1)
     relay_three = swap_y(far_low, 3)

time: 95.5 us -> 94.7 us (level)
  waiting for transfers between devices: 20.8 us -> 19.2 us
  Pallas kernels: 9.71 us -> 10.7 us
    pallas_call x1 -> x2, Pallas kernels: 0.66 us -> 2.15 us  [the longest x1 2.06 us: own_far_product(): pl.pallas_call(body, in_specs=[pl.BlockSpec(memory_space=pltpu.SMEM), pl....]
    ppermute x2, waiting for transfers between devices: 1.33 us -> 0.01 us  [swap_core(): return lax.ppermute(x, 'mp', [(i, i ^ 1) for i in range(n)])]
  transfers between devices with their start and end apart: 13 -> 13, of which waited for: 6 -> 5; matrix products, arithmetic and copies ran while one was open for 0% -> 0% of each run, Pallas kernels for 4% -> 6%
where the time goes in v3:
time: 94.7 us; the launch traced here: 94.1 us
  starting transfers between devices  63.3 us (67%)
  waiting for transfers between devices  19.2 us (20%)
  Pallas kernels  10.7 us (11%)
    ppermute x6, starting transfers between devices, swap_y(): return lax.ppermute(x, 'mp', [(i, i ^ 2 * pair) for i in range(n)])  21.2 us
    ppermute x2, starting transfers between devices, swap_core(): return lax.ppermute(x, 'mp', [(i, i ^ 1) for i in range(n)])  14.4 us
    ppermute x3, starting transfers between devices, along_section(): return lax.ppermute(x, 'section', [(i, (i + by) % n) for i in range(n)])  13.6 us
    all_to_all x1, starting transfers between devices, local(): lax.all_to_all(partial_sums(got, scaled, lax.axis_size('mp')), 'mp', spli...  10.1 us
    ppermute x3, waiting for transfers between devices, along_section(): return lax.ppermute(x, 'section', [(i, (i + by) % n) for i in range(n)])  8.09 us
    all_to_all x1, waiting for transfers between devices, local(): lax.all_to_all(partial_sums(got, scaled, lax.axis_size('mp')), 'mp', spli...  5.29 us
    all_to_all x1, starting transfers between devices, local(): lax.all_to_all(section_out, 'dp', split_axis=0, concat_axis=0, tiled=True)  4.02 us
    all_to_all x1, waiting for transfers between devices, local(): lax.all_to_all(section_out, 'dp', split_axis=0, concat_axis=0, tiled=True)  3.99 us
  transfers between devices with their start and end apart: 13, of which 5 were waited for; matrix products, arithmetic and copies ran while one was open for 0% of the time, Pallas kernels for 6%

profile of v3, /device:TPU:1, one launch (start us, length us, event | category | flops | bytes accessed | tf_op | source)
XLA Modules:
  0.0 94.1 jit_solution(15131579405989124033)
XLA Ops:
  0.6 2.1 %far_product.1 = (bf16[8,192,128]{2,1,0:T(8,128)(2,1)S(1)}, bf16[1024,768]{1,0:T(8,128)(2,1)S(1)}) custom-call(s32[1]{0:T(128)} %bitcast.me_ref, bf16[8,192,768]{2,1,0:T(8,128)(2,1)} %bitcast.13, bf16[1024,768]{1,0:T(8,128)(2,1)} %bitcast.15), custom_call_target="tpu_custom_call" | custom-call | flops 301989888 | bytes 2654208 | tf_op jit(solution)/shard_map/far_product/pallas_call | solution.py:76
  2.8 12.4 %collective-permute-start = (bf16[8,192,128]{2,1,0:T(8,128)(2,1)S(1)}, bf16[8,192,128]{2,1,0:T(8,128)(2,1)S(1)}, u32[]{:S(2)}, u32[]{:S(2)}) collective-permute-start(bf16[8,192,128]{2,1,0:T(8,128)(2,1)S(1)} %get-tuple-element.22), channel_id=1, source_target_pairs={{0,8},{8,0},{16,24},{24,16},{32,40},{40,32},{48,56},{56,48},{1,9},... | collective-permute-start | bytes 1179656 | tf_op jit(solution)/shard_map/ppermute | solution.py:19
  15.2 2.1 %own_far_product.1 = (f32[8,192,128]{2,1,0:T(8,128)S(1)}, bf16[576,768]{1,0:T(8,128)(2,1)S(1)}, bf16[576,768]{1,0:T(8,128)(2,1)S(1)}) custom-call(s32[1]{0:T(128)} %bitcast.me_ref, bf16[8,192,768]{2,1,0:T(8,128)(2,1)} %bitcast.14, bf16[1024,768]{1,0:T(8,128)(2,1)S(1)} %get-tuple-element.18.c_ref), custom_call_target="tpu_custom_call" | custom-call | flops 603979776 | bytes 3735552 | tf_op jit(solution)/shard_map/own_far_product/pallas_call | solution.py:107
  17.3 0.0 collective-permute-done.other_ref
  17.3 0.1 far_sum.1
  17.4 0.0 copy-start.1
  17.4 1.1 %near_product.1 = bf16[3,8,192,128]{3,2,1,0:T(8,128)(2,1)S(1)} custom-call(bf16[576,768]{1,0:T(8,128)(2,1)S(1)} %get-tuple-element.20.w_ref, bf16[1024,768]{1,0:T(8,128)(2,1)S(1)} %get-tuple-element.18.c_ref, bf16[8,96,128]{2,1,0:T(8,128)(2,1)S(1)} %get-tuple-element.23.after_ref), custom_call_target="tpu_custom_call" | custom-call | flops 905969664 | bytes 4816896 | tf_op jit(solution)/shard_map/near_product/pallas_call | solution.py:128
  18.5 1.9 %collective-permute-start.1 = (bf16[3,8,192,128]{3,2,1,0:T(8,128)(2,1)S(1)}, bf16[3,8,192,128]{3,2,1,0:T(8,128)(2,1)S(1)}, u32[]{:S(2)}, u32[]{:S(2)}) collective-permute-start(bf16[3,8,192,128]{3,2,1,0:T(8,128)(2,1)S(1)} %near_product.1), channel_id=1, source_target_pairs={{0,8},{8,0},{16,24},{24,16},{32,40},{40,32},{48,56},{56,48},{1,9},... | collective-permute-start | bytes 3538952 | tf_op jit(solution)/shard_map/ppermute | solution.py:19
  20.5 1.9 %collective-permute-start.5 = (bf16[8,96,128]{2,1,0:T(8,128)(2,1)S(1)}, bf16[8,96,128]{2,1,0:T(8,128)(2,1)S(1)}, u32[]{:S(2)}, u32[]{:S(2)}) collective-permute-start(bf16[8,96,128]{2,1,0:T(8,128)(2,1)S(1)} %get-tuple-element.30), channel_id=1, source_target_pairs={{0,48},{8,56},{16,32},{24,40},{32,16},{40,24},{48,0},{56,8},{1,49}... | collective-permute-start | bytes 589832 | tf_op jit(solution)/shard_map/ppermute | solution.py:24
  22.4 1.9 %collective-permute-start.4 = (bf16[8,96,128]{2,1,0:T(8,128)(2,1)S(1)}, bf16[8,96,128]{2,1,0:T(8,128)(2,1)S(1)}, u32[]{:S(2)}, u32[]{:S(2)}) collective-permute-start(bf16[8,96,128]{2,1,0:T(8,128)(2,1)S(1)} %get-tuple-element.23.after_ref), channel_id=1, source_target_pairs={{0,16},{8,24},{16,0},{24,8},{32,48},{40,56},{48,32},{56,40},{1,17}... | collective-permute-start | bytes 589832 | tf_op jit(solution)/shard_map/ppermute | solution.py:24
  24.3 0.0 collective-permute-done.1.r_ref
  24.3 0.0 copy-done.1
  24.3 0.0 copy-start
  24.3 0.0 copy-start.2
  24.4 1.1 %near_sum.1 = (bf16[8,96,128]{2,1,0:T(8,128)(2,1)S(1)}, bf16[8,96,128]{2,1,0:T(8,128)(2,1)S(1)}, f32[8,96,128]{2,1,0:T(8,128)S(1)}, f32[8,96,128]{2,1,0:T(8,128)S(1)}, f32[8,192,128]{2,1,0:T(8,128)S(1)}) custom-call(bf16[576,768]{1,0:T(8,128)(2,1)S(1)} %get-tuple-element.19.w_ref, bf16[1024,768]{1,0:T(8,128)(2,1)S(1)} %get-tuple-element.18.c_ref, ...), custom_call_target="tpu_custom_call" | custom-call | flops 905969664 | bytes 4816896 | tf_op jit(solution)/shard_map/near_sum/pallas_call | solution.py:168
  25.5 4.3 %collective-permute-start.2 = (bf16[8,96,128]{2,1,0:T(8,128)(2,1)S(1)}, bf16[8,96,128]{2,1,0:T(8,128)(2,1)S(1)}, u32[]{:S(2)}, u32[]{:S(2)}) collective-permute-start(bf16[8,96,128]{2,1,0:T(8,128)(2,1)S(1)} %get-tuple-element.25), channel_id=1, source_target_pairs={{0,16},{8,24},{16,0},{24,8},{32,48},{40,56},{48,32},{56,40},{1,17}... | collective-permute-start | bytes 589832 | tf_op jit(solution)/shard_map/ppermute | solution.py:24
  29.8 5.5 %collective-permute-start.3 = (bf16[8,96,128]{2,1,0:T(8,128)(2,1)S(1)}, bf16[8,96,128]{2,1,0:T(8,128)(2,1)S(1)}, u32[]{:S(2)}, u32[]{:S(2)}) collective-permute-start(bf16[8,96,128]{2,1,0:T(8,128)(2,1)S(1)} %get-tuple-element.26), channel_id=1, source_target_pairs={{0,48},{8,56},{16,32},{24,40},{32,16},{40,24},{48,0},{56,8},{1,49}... | collective-permute-start | bytes 589832 | tf_op jit(solution)/shard_map/ppermute | solution.py:24
  35.2 0.0 collective-permute-done.5.from_three_ref
  35.2 1.8 %collective-permute-done.4.from_one_ref = bf16[8,96,128]{2,1,0:T(8,128)(2,1)S(1)} collective-permute-done((bf16[8,96,128]{2,1,0:T(8,128)(2,1)S(1)}, bf16[8,96,128]{2,1,0:T(8,128)(2,1)S(1)}, u32[]{:S(2)}, u32[]{:S(2)}) %collective-permute-start.4) | collective-permute-done | bytes 196640 | tf_op jit(solution)/shard_map/ppermute | solution.py:24
  37.0 0.1 relay_sum.1
  37.1 5.7 %collective-permute-start.6 = (bf16[8,96,128]{2,1,0:T(8,128)(2,1)S(1)}, bf16[8,96,128]{2,1,0:T(8,128)(2,1)S(1)}, u32[]{:S(2)}, u32[]{:S(2)}) collective-permute-start(bf16[8,96,128]{2,1,0:T(8,128)(2,1)S(1)} %get-tuple-element.31), channel_id=1, source_target_pairs={{0,48},{8,56},{16,32},{24,40},{32,16},{40,24},{48,0},{56,8},{1,49}... | collective-permute-start | bytes 589832 | tf_op jit(solution)/shard_map/ppermute | solution.py:24
  42.8 1.9 %collective-permute-start.7 = (bf16[8,96,128]{2,1,0:T(8,128)(2,1)S(1)}, bf16[8,96,128]{2,1,0:T(8,128)(2,1)S(1)}, u32[]{:S(2)}, u32[]{:S(2)}) collective-permute-start(bf16[8,96,128]{2,1,0:T(8,128)(2,1)S(1)} %get-tuple-element.32), channel_id=1, source_target_pairs={{0,16},{8,24},{16,0},{24,8},{32,48},{40,56},{48,32},{56,40},{1,17}... | collective-permute-start | bytes 589832 | tf_op jit(solution)/shard_map/ppermute | solution.py:24
  44.7 0.0 collective-permute-done.2.top_ref
  44.7 0.0 collective-permute-done.3.low_ref
  44.7 0.0 copy-done
  44.7 0.0 copy-done.2
  44.7 0.1 add_direct.1
  44.9 9.7 %collective-permute-start.9 = (bf16[144,1536]{1,0:T(8,128)(2,1)S(1)}, bf16[144,1536]{1,0:T(8,128)(2,1)S(1)}, u32[]{:S(2)}, u32[]{:S(2)}) collective-permute-start(bf16[144,1536]{1,0:T(8,128)(2,1)S(1)} %get-tuple-element.33), channel_id=1, source_target_pairs={{0,704},{64,0},{128,64},{192,128},{256,192},{320,256},{384,320},{4... | collective-permute-start | bytes 1327112 | tf_op jit(solution)/shard_map/ppermute | solution.py:29
  54.6 0.0 collective-permute-done.6.top_ref
  54.6 0.0 collective-permute-done.7.low_ref
  54.6 0.8 add_last.1
  55.4 4.0 %all-to-all-start = ((bf16[8,192,128]{2,1,0:T(8,128)(2,1)}), bf16[8,192,128]{2,1,0:T(8,128)(2,1)S(1)}, u32[]{:S(2)}, u32[]{:S(2)}) async-start(bf16[8,192,128]{2,1,0:T(8,128)(2,1)} %add_last.1), calls=%async_computation | async-start | bytes 786432 | tf_op jit(solution)/shard_map/all_to_all | solution.py:315
  59.5 2.6 %collective-permute-done.9.pack_ref = bf16[144,1536]{1,0:T(8,128)(2,1)S(1)} collective-permute-done((bf16[144,1536]{1,0:T(8,128)(2,1)S(1)}, bf16[144,1536]{1,0:T(8,128)(2,1)S(1)}, u32[]{:S(2)}, u32[]{:S(2)}) %collective-permute-start.9) | collective-permute-done | bytes 442400 | tf_op jit(solution)/shard_map/ppermute | solution.py:29
  62.0 0.3 scaled_cotangent.1.s_ref
  62.3 4.0 %all-to-all-done.x_ref = bf16[8,192,128]{2,1,0:T(8,128)(2,1)S(1)} async-done(((bf16[8,192,128]{2,1,0:T(8,128)(2,1)}), bf16[8,192,128]{2,1,0:T(8,128)(2,1)S(1)}, u32[]{:S(2)}, u32[]{:S(2)}) %all-to-all-start) | async-done | bytes 393248 | tf_op jit(solution)/shard_map/all_to_all | solution.py:315
  66.3 0.9 partial_sums.1
  67.2 10.1 %all-to-all-start.1 = ((f32[8,8,128]{2,1,0:T(8,128)}), f32[8,8,128]{2,1,0:T(8,128)S(1)}, u32[]{:S(2)}, u32[]{:S(2)}) async-start(f32[8,8,128]{2,1,0:T(8,128)} %partial_sums.1), calls=%async_computation.1 | async-start | bytes 65536 | tf_op jit(solution)/shard_map/all_to_all | solution.py:319
  77.3 1.9 %collective-permute-start.8 = (bf16[8,192,128]{2,1,0:T(8,128)(2,1)S(1)}, bf16[8,192,128]{2,1,0:T(8,128)(2,1)S(1)}, u32[]{:S(2)}, u32[]{:S(2)}) collective-permute-start(bf16[8,192,128]{2,1,0:T(8,128)(2,1)S(1)} %all-to-all-done.x_ref), channel_id=1, source_target_pairs={{0,64},{64,128},{128,192},{192,256},{256,320},{320,384},{384,448},... | collective-permute-start | bytes 1179656 | tf_op jit(solution)/shard_map/ppermute | solution.py:29
  79.2 5.3 %all-to-all-done.1.s_ref = f32[8,8,128]{2,1,0:T(8,128)S(1)} async-done(((f32[8,8,128]{2,1,0:T(8,128)}), f32[8,8,128]{2,1,0:T(8,128)S(1)}, u32[]{:S(2)}, u32[]{:S(2)}) %all-to-all-start.1) | async-done | bytes 32800 | tf_op jit(solution)/shard_map/all_to_all | solution.py:319
  84.5 0.0 copy-start.3
  84.5 1.9 %collective-permute-start.10 = (f32[8,128]{1,0:T(8,128)S(1)}, f32[8,128]{1,0:T(8,128)S(1)}, u32[]{:S(2)}, u32[]{:S(2)}) collective-permute-start(f32[8,128]{1,0:T(8,128)S(1)} %statistics.1.st_ref), channel_id=1, source_target_pairs={{0,64},{64,128},{128,192},{192,256},{256,320},{320,384},{384,448},... | collective-permute-start | bytes 12296 | tf_op jit(solution)/shard_map/ppermute | solution.py:29
  86.5 1.0 %gradient.1 = bf16[128,1536]{1,0:T(8,128)(2,1)} custom-call(bf16[8,192,128]{2,1,0:T(8,128)(2,1)S(1)} %all-to-all-done.x_ref, f32[1536,128]{1,0:T(8,128)S(1)} %scaled_cotangent.1.s_ref, f32[8,128]{1,0:T(8,128)S(1)} %statistics.1.st_ref), custom_call_target="tpu_custom_call" | custom-call | flops 11796480000 | bytes 1183744 | tf_op jit(solution)/shard_map/gradient/pallas_call | solution.py:227
  87.5 5.5 %collective-permute-done.10.st_ref = f32[8,128]{1,0:T(8,128)S(1)} collective-permute-done((f32[8,128]{1,0:T(8,128)S(1)}, f32[8,128]{1,0:T(8,128)S(1)}, u32[]{:S(2)}, u32[]{:S(2)}) %collective-permute-start.10) | collective-permute-done | bytes 4128 | tf_op jit(solution)/shard_map/ppermute | solution.py:29
  93.0 0.0 collective-permute-done.8.x_ref
  93.0 0.0 copy-done.3
  93.0 1.0 %layer_norm.1 = bf16[128,1536]{1,0:T(8,128)(2,1)} custom-call(bf16[8,192,128]{2,1,0:T(8,128)(2,1)S(1)} %collective-permute-done.8.x_ref, f32[8,128]{1,0:T(8,128)S(1)} %collective-permute-done.10.st_ref, f32[1,1536]{1,0:T(1,128)S(1)} %copy-done.2, f32[1,1536]{1,0:T(1,128)S(1)} %copy-done.3), custom_call_target="tpu_custom_call" | custom-call | flops 786432 | bytes 409600 | tf_op jit(solution)/shard_map/layer_norm/pallas_call | solution.py:227
  (3 shorter events, 0.0 us)
Async XLA Ops:
  2.8 14.5 %collective-permute-start = (bf16[8,192,128]{2,1,0:T(8,128)(2,1)S(1)}, bf16[8,192,128]{2,1,0:T(8,128)(2,1)S(1)}, u32[]{:S(2)}, u32[]{:S(2)}) collective-permute-start(bf16[8,192,128]{2,1,0:T(8,128)(2,1)S(1)} %get-tuple-element.22), channel_id=1, source_target_pairs={{0,8},{8,0},{16,24},{24,16},{32,40},{40,32},{48,56},{56,48},{1,9},... | collective-permute-start | bytes 1179656 | tf_op jit(solution)/shard_map/ppermute | solution.py:19
  17.4 6.9 %copy-start.1 = (bf16[1,1024,192]{1,2,0:T(8,128)(2,1)S(1)}, bf16[1,1024,192]{1,2,0:T(8,128)(2,1)}, u32[]{:S(2)}) copy-start(bf16[1,1024,192]{1,2,0:T(8,128)(2,1)} %param.8) | copy-start | bytes 1179652
  18.5 5.8 %collective-permute-start.1 = (bf16[3,8,192,128]{3,2,1,0:T(8,128)(2,1)S(1)}, bf16[3,8,192,128]{3,2,1,0:T(8,128)(2,1)S(1)}, u32[]{:S(2)}, u32[]{:S(2)}) collective-permute-start(bf16[3,8,192,128]{3,2,1,0:T(8,128)(2,1)S(1)} %near_product.1), channel_id=1, source_target_pairs={{0,8},{8,0},{16,24},{24,16},{32,40},{40,32},{48,56},{56,48},{1,9},... | collective-permute-start | bytes 3538952 | tf_op jit(solution)/shard_map/ppermute | solution.py:19
  20.5 14.8 %collective-permute-start.5 = (bf16[8,96,128]{2,1,0:T(8,128)(2,1)S(1)}, bf16[8,96,128]{2,1,0:T(8,128)(2,1)S(1)}, u32[]{:S(2)}, u32[]{:S(2)}) collective-permute-start(bf16[8,96,128]{2,1,0:T(8,128)(2,1)S(1)} %get-tuple-element.30), channel_id=1, source_target_pairs={{0,48},{8,56},{16,32},{24,40},{32,16},{40,24},{48,0},{56,8},{1,49}... | collective-permute-start | bytes 589832 | tf_op jit(solution)/shard_map/ppermute | solution.py:24
  22.4 14.6 %collective-permute-start.4 = (bf16[8,96,128]{2,1,0:T(8,128)(2,1)S(1)}, bf16[8,96,128]{2,1,0:T(8,128)(2,1)S(1)}, u32[]{:S(2)}, u32[]{:S(2)}) collective-permute-start(bf16[8,96,128]{2,1,0:T(8,128)(2,1)S(1)} %get-tuple-element.23.after_ref), channel_id=1, source_target_pairs={{0,16},{8,24},{16,0},{24,8},{32,48},{40,56},{48,32},{56,40},{1,17}... | collective-permute-start | bytes 589832 | tf_op jit(solution)/shard_map/ppermute | solution.py:24
  24.3 20.4 %copy-start = (bf16[1,128,1536]{2,1,0:T(8,128)(2,1)S(1)}, bf16[1,128,1536]{2,1,0:T(8,128)(2,1)}, u32[]{:S(2)}) copy-start(bf16[1,128,1536]{2,1,0:T(8,128)(2,1)} %param.11) | copy-start | bytes 1179652
  24.3 20.4 %copy-start.2 = (f32[1,1536]{1,0:T(1,128)S(1)}, f32[1,1536]{1,0:T(1,128)}, u32[]{:S(2)}) copy-start(f32[1,1536]{1,0:T(1,128)} %g_ref.1) | copy-start | bytes 18436
  25.5 19.2 %collective-permute-start.2 = (bf16[8,96,128]{2,1,0:T(8,128)(2,1)S(1)}, bf16[8,96,128]{2,1,0:T(8,128)(2,1)S(1)}, u32[]{:S(2)}, u32[]{:S(2)}) collective-permute-start(bf16[8,96,128]{2,1,0:T(8,128)(2,1)S(1)} %get-tuple-element.25), channel_id=1, source_target_pairs={{0,16},{8,24},{16,0},{24,8},{32,48},{40,56},{48,32},{56,40},{1,17}... | collective-permute-start | bytes 589832 | tf_op jit(solution)/shard_map/ppermute | solution.py:24
  29.8 15.0 %collective-permute-start.3 = (bf16[8,96,128]{2,1,0:T(8,128)(2,1)S(1)}, bf16[8,96,128]{2,1,0:T(8,128)(2,1)S(1)}, u32[]{:S(2)}, u32[]{:S(2)}) collective-permute-start(bf16[8,96,128]{2,1,0:T(8,128)(2,1)S(1)} %get-tuple-element.26), channel_id=1, source_target_pairs={{0,48},{8,56},{16,32},{24,40},{32,16},{40,24},{48,0},{56,8},{1,49}... | collective-permute-start | bytes 589832 | tf_op jit(solution)/shard_map/ppermute | solution.py:24
  37.1 17.5 %collective-permute-start.6 = (bf16[8,96,128]{2,1,0:T(8,128)(2,1)S(1)}, bf16[8,96,128]{2,1,0:T(8,128)(2,1)S(1)}, u32[]{:S(2)}, u32[]{:S(2)}) collective-permute-start(bf16[8,96,128]{2,1,0:T(8,128)(2,1)S(1)} %get-tuple-element.31), channel_id=1, source_target_pairs={{0,48},{8,56},{16,32},{24,40},{32,16},{40,24},{48,0},{56,8},{1,49}... | collective-permute-start | bytes 589832 | tf_op jit(solution)/shard_map/ppermute | solution.py:24
  42.8 11.9 %collective-permute-start.7 = (bf16[8,96,128]{2,1,0:T(8,128)(2,1)S(1)}, bf16[8,96,128]{2,1,0:T(8,128)(2,1)S(1)}, u32[]{:S(2)}, u32[]{:S(2)}) collective-permute-start(bf16[8,96,128]{2,1,0:T(8,128)(2,1)S(1)} %get-tuple-element.32), channel_id=1, source_target_pairs={{0,16},{8,24},{16,0},{24,8},{32,48},{40,56},{48,32},{56,40},{1,17}... | collective-permute-start | bytes 589832 | tf_op jit(solution)/shard_map/ppermute | solution.py:24
  44.9 17.2 %collective-permute-start.9 = (bf16[144,1536]{1,0:T(8,128)(2,1)S(1)}, bf16[144,1536]{1,0:T(8,128)(2,1)S(1)}, u32[]{:S(2)}, u32[]{:S(2)}) collective-permute-start(bf16[144,1536]{1,0:T(8,128)(2,1)S(1)} %get-tuple-element.33), channel_id=1, source_target_pairs={{0,704},{64,0},{128,64},{192,128},{256,192},{320,256},{384,320},{4... | collective-permute-start | bytes 1327112 | tf_op jit(solution)/shard_map/ppermute | solution.py:29
  55.4 10.9 %all-to-all-start = ((bf16[8,192,128]{2,1,0:T(8,128)(2,1)}), bf16[8,192,128]{2,1,0:T(8,128)(2,1)S(1)}, u32[]{:S(2)}, u32[]{:S(2)}) async-start(bf16[8,192,128]{2,1,0:T(8,128)(2,1)} %add_last.1), calls=%async_computation | async-start | bytes 786432 | tf_op jit(solution)/shard_map/all_to_all | solution.py:315
  67.2 17.3 %all-to-all-start.1 = ((f32[8,8,128]{2,1,0:T(8,128)}), f32[8,8,128]{2,1,0:T(8,128)S(1)}, u32[]{:S(2)}, u32[]{:S(2)}) async-start(f32[8,8,128]{2,1,0:T(8,128)} %partial_sums.1), calls=%async_computation.1 | async-start | bytes 65536 | tf_op jit(solution)/shard_map/all_to_all | solution.py:319
  77.3 15.7 %collective-permute-start.8 = (bf16[8,192,128]{2,1,0:T(8,128)(2,1)S(1)}, bf16[8,192,128]{2,1,0:T(8,128)(2,1)S(1)}, u32[]{:S(2)}, u32[]{:S(2)}) collective-permute-start(bf16[8,192,128]{2,1,0:T(8,128)(2,1)S(1)} %all-to-all-done.x_ref), channel_id=1, source_target_pairs={{0,64},{64,128},{128,192},{192,256},{256,320},{320,384},{384,448},... | collective-permute-start | bytes 1179656 | tf_op jit(solution)/shard_map/ppermute | solution.py:29
  84.5 8.5 %copy-start.3 = (f32[1,1536]{1,0:T(1,128)S(1)}, f32[1,1536]{1,0:T(1,128)}, u32[]{:S(2)}) copy-start(f32[1,1536]{1,0:T(1,128)} %b_ref.1) | copy-start | bytes 18436
  84.5 8.5 %collective-permute-start.10 = (f32[8,128]{1,0:T(8,128)S(1)}, f32[8,128]{1,0:T(8,128)S(1)}, u32[]{:S(2)}, u32[]{:S(2)}) collective-permute-start(f32[8,128]{1,0:T(8,128)S(1)} %statistics.1.st_ref), channel_id=1, source_target_pairs={{0,64},{64,128},{128,192},{192,256},{256,320},{320,384},{384,448},... | collective-permute-start | bytes 12296 | tf_op jit(solution)/shard_map/ppermute | solution.py:29

commit v4 on v3

--- a/solution.py
+++ b/solution.py
@@ -49,37 +49,34 @@
     return (((me >> 1) ^ order) << 1) + core
 
 
-def far_product(me, weights, ctx):
+def sent_products(me, weights, ctx):
     rows, depth = weights.shape[1:]
     toks = ctx.shape[0]
     n_parts = 4
 
-    def body(me_ref, w_ref, c_ref, far_ref, ctx_ref, far_w, c_sem, w_sem):
+    def body(me_ref, w_ref, c_ref, sent_ref, ctx_ref, sent_w, c_sem, w_sem):
         me = me_ref[0]
-
-        def c_copy(i):
+        copies = [pltpu.make_async_copy(w_ref.at[block_of(me, ORDER[k], 1 - (me & 1))], sent_w.at[pl.ds(k * rows, rows)], w_sem.at[k]) for k in range(4)]
+        for i in range(n_parts):
             part = pl.ds(i * (toks // n_parts), toks // n_parts)
-            return pltpu.make_async_copy(c_ref.at[part], ctx_ref.at[part], c_sem.at[i])
-
-        w_copy = pltpu.make_async_copy(w_ref.at[block_of(me, ORDER[0], 1 - (me & 1))], far_w, w_sem)
-        w_copy.start()
-        for i in range(n_parts):
-            c_copy(i).start()
-        w_copy.wait()
-        for i in range(n_parts):
-            c_copy(i).wait()
+            copies.append(pltpu.make_async_copy(c_ref.at[part], ctx_ref.at[part], c_sem.at[i]))
+        for copy in copies:
+            copy.start()
+        for copy in copies:
+            copy.wait()
         for i in range(toks // (STEP * TB)):
-            acc = dot_t(far_w[...], ctx_ref[pl.ds(i * STEP * TB, STEP * TB)])
+            acc = dot_t(sent_w[...], ctx_ref[pl.ds(i * STEP * TB, STEP * TB)])
             for b in range(STEP):
-                far_ref[STEP * i + b] = acc[:, b * TB:(b + 1) * TB].astype(BF16)
+                for k in range(4):
+                    sent_ref[k, STEP * i + b] = acc[k * rows:(k + 1) * rows, b * TB:(b + 1) * TB].astype(BF16)
 
     return pl.pallas_call(
         body,
         in_specs=[pl.BlockSpec(memory_space=pltpu.SMEM), pl.BlockSpec(memory_space=pltpu.HBM), pl.BlockSpec(memory_space=pltpu.HBM)],
         out_specs=vmem(2),
-        out_shape=(jax.ShapeDtypeStruct((toks // TB, rows, TB), BF16), jax.ShapeDtypeStruct((toks, depth), BF16)),
-        scratch_shapes=[pltpu.VMEM((rows, depth), BF16), pltpu.SemaphoreType.DMA((n_parts,)), pltpu.SemaphoreType.DMA],
-        compiler_params=params(16), cost_estimate=cost(1, rows, depth, toks), name="far_product",
+        out_shape=(jax.ShapeDtypeStruct((4, toks // TB, rows, TB), BF16), jax.ShapeDtypeStruct((toks, depth), BF16)),
+        scratch_shapes=[pltpu.VMEM((4 * rows, depth), BF16), pltpu.SemaphoreType.DMA((n_parts,)), pltpu.SemaphoreType.DMA((4,))],
+        compiler_params=params(16), cost_estimate=cost(4, rows, depth, toks), name="sent_products",
     )(me, weights, ctx)
 
 
@@ -87,12 +84,11 @@
     rows, depth = weights.shape[1:]
     toks = ctx.shape[0]
 
-    def body(me_ref, w_ref, c_ref, far_ref, near_w_ref, own_w_ref, far_w, far_sem, near_sem, own_sem):
+    def body(me_ref, w_ref, c_ref, far_ref, own_w_ref, far_w, far_sem, own_sem):
         me = me_ref[0]
         core = me & 1
         far_copy = pltpu.make_async_copy(w_ref.at[block_of(me, ORDER[0], core)], far_w, far_sem)
-        copies = [pltpu.make_async_copy(w_ref.at[block_of(me, ORDER[k], 1 - core)], near_w_ref.at[pl.ds((k - 1) * rows, rows)], near_sem.at[k - 1]) for k in range(1, 4)]
-        copies += [pltpu.make_async_copy(w_ref.at[block_of(me, ORDER[k], core)], own_w_ref.at[pl.ds((k - 1) * rows, rows)], own_sem.at[k - 1]) for k in range(1, 4)]
+        copies = [pltpu.make_async_copy(w_ref.at[block_of(me, ORDER[k], core)], own_w_ref.at[pl.ds((k - 1) * rows, rows)], own_sem.at[k - 1]) for k in range(1, 4)]
         far_copy.start()
         for copy in copies:
             copy.start()
@@ -107,36 +103,19 @@
     return pl.pallas_call(
         body,
         in_specs=[pl.BlockSpec(memory_space=pltpu.SMEM), pl.BlockSpec(memory_space=pltpu.HBM), *vmem(1)],
-        out_specs=vmem(3),
-        out_shape=(jax.ShapeDtypeStruct((toks // TB, rows, TB), F32), jax.ShapeDtypeStruct((3 * rows, depth), BF16), jax.ShapeDtypeStruct((3 * rows, depth), BF16)),
-        scratch_shapes=[pltpu.VMEM((rows, depth), BF16), pltpu.SemaphoreType.DMA, pltpu.SemaphoreType.DMA((3,)), pltpu.SemaphoreType.DMA((3,))],
+        out_specs=vmem(2),
+        out_shape=(jax.ShapeDtypeStruct((toks // TB, rows, TB), F32), jax.ShapeDtypeStruct((3 * rows, depth), BF16)),
+        scratch_shapes=[pltpu.VMEM((rows, depth), BF16), pltpu.SemaphoreType.DMA, pltpu.SemaphoreType.DMA((3,))],
         compiler_params=params(16), cost_estimate=cost(2, rows, depth, toks), name="own_far_product",
     )(me, weights, ctx)
 
 
-def near_product(weights, ctx, after):
-    toks, depth = ctx.shape
-    rows = weights.shape[0] // 3
-
-    def body(w_ref, c_ref, after_ref, o_ref):
-        for i in range(toks // (STEP * TB)):
-            acc = dot_t(w_ref[...], c_ref[pl.ds(i * STEP * TB, STEP * TB)])
-            for b in range(STEP):
-                for k in range(3):
-                    o_ref[k, STEP * i + b] = acc[k * rows:(k + 1) * rows, b * TB:(b + 1) * TB].astype(BF16)
-
-    return pl.pallas_call(
-        body, in_specs=[*vmem(2), pl.BlockSpec(memory_space=pl.ANY)], out_specs=vmem(1)[0], out_shape=jax.ShapeDtypeStruct((3, toks // TB, rows, TB), BF16),
-        compiler_params=params(16), cost_estimate=cost(3, rows, depth, toks), name="near_product",
-    )(weights, ctx, after)
-
-
 def far_sum(own, other):
     half = own.shape[1] // 2
 
     def body(own_ref, other_ref, top_ref, low_ref):
-        top_ref[...] = (own_ref[:, :half] + other_ref[:, :half].astype(F32)).astype(BF16)
-        low_ref[...] = (own_ref[:, half:] + other_ref[:, half:].astype(F32)).astype(BF16)
+        top_ref[...] = (own_ref[:, :half] + other_ref[0, :, :half].astype(F32)).astype(BF16)
+        low_ref[...] = (own_ref[:, half:] + other_ref[0, :, half:].astype(F32)).astype(BF16)
 
     shape = jax.ShapeDtypeStruct((own.shape[0], half, own.shape[2]), BF16)
     return pl.pallas_call(
@@ -156,13 +135,13 @@
             for b in range(STEP):
                 t = STEP * i + b
                 cut = slice(b * TB, (b + 1) * TB)
-                one = acc[:rows, cut] + r_ref[0, t].astype(F32)
+                one = acc[:rows, cut] + r_ref[1, t].astype(F32)
                 one_ref[t] = one[:half].astype(BF16)
                 keep_one_ref[t] = one[half:]
-                three = acc[rows:2 * rows, cut] + r_ref[1, t].astype(F32)
+                three = acc[rows:2 * rows, cut] + r_ref[2, t].astype(F32)
                 three_ref[t] = three[half:].astype(BF16)
                 keep_three_ref[t] = three[:half]
-                mine_ref[t] = acc[2 * rows:, cut] + r_ref[2, t].astype(F32) + res_ref[:, t * TB:(t + 1) * TB].astype(F32)
+                mine_ref[t] = acc[2 * rows:, cut] + r_ref[3, t].astype(F32) + res_ref[:, t * TB:(t + 1) * TB].astype(F32)
 
     part = lambda dtype: jax.ShapeDtypeStruct((toks // TB, half, TB), dtype)
     return pl.pallas_call(
@@ -296,14 +275,13 @@
     weights = pltpu.with_memory_space_constraint(weights, pltpu.HBM)
     ctx = pltpu.with_memory_space_constraint(context[0], pltpu.HBM)
 
-    far_sent, ctx = far_product(m.reshape(1), weights, ctx)
-    far_got = swap_core(far_sent)
-    far_own, near_weights, own_weights = own_far_product(m.reshape(1), weights, ctx)
-    far_top, far_low = far_sum(far_own, far_got)
-    near_got = swap_core(near_product(near_weights, ctx, far_top))
+    sent, ctx = sent_products(m.reshape(1), weights, ctx)
+    got = swap_core(sent)
+    far_own, own_weights = own_far_product(m.reshape(1), weights, ctx)
+    far_top, far_low = far_sum(far_own, got)
     relay_one = swap_y(far_top, 1)
     relay_three = swap_y(far_low, 3)
-    one, three, keep_one, keep_three, mine = near_sum(own_weights, ctx, near_got, residual[0].T)
+    one, three, keep_one, keep_three, mine = near_sum(own_weights, ctx, got, residual[0].T)
     direct_one = swap_y(one, 1)
     direct_three = swap_y(three, 3)
     on_one, on_three = relay_sum(keep_one, keep_three, relay_one, relay_three)

time: 94.7 us -> 94.9 us (level)
  waiting for transfers between devices: 19.2 us -> 22.4 us
  starting transfers between devices: 63.3 us -> 60.5 us
    all_to_all x1, waiting for transfers between devices: 3.99 us -> 7.24 us  [local(): lax.all_to_all(section_out, 'dp', split_axis=0, concat_axis=0, tiled=True)]
    ppermute x3, waiting for transfers between devices: 8.09 us -> 5.1 us  [along_section(): return lax.ppermute(x, 'section', [(i, (i + by) % n) for i in range(n)])]
    all_to_all x1, starting transfers between devices: 10.1 us -> 7.18 us  [local(): lax.all_to_all(partial_sums(got, scaled, lax.axis_size('mp')), 'mp', spli...]
    all_to_all x1, starting transfers between devices: 4.02 us -> 6.33 us  [local(): lax.all_to_all(section_out, 'dp', split_axis=0, concat_axis=0, tiled=True)]
    ppermute x2 -> x1, starting transfers between devices: 14.4 us -> 12.4 us  [swap_core(): return lax.ppermute(x, 'mp', [(i, i ^ 1) for i in range(n)])]
    ppermute x6, starting transfers between devices: 21.2 us -> 19.3 us  [swap_y(): return lax.ppermute(x, 'mp', [(i, i ^ 2 * pair) for i in range(n)])]
    ppermute x6, waiting for transfers between devices: 1.77 us -> 3.63 us  [swap_y(): return lax.ppermute(x, 'mp', [(i, i ^ 2 * pair) for i in range(n)])]
    ppermute x3, starting transfers between devices: 13.6 us -> 15.4 us  [along_section(): return lax.ppermute(x, 'section', [(i, (i + by) % n) for i in range(n)])]
  transfers between devices with their start and end apart: 13 -> 12, of which waited for: 5 -> 6; matrix products, arithmetic and copies ran while one was open for 0% -> 0% of each run, Pallas kernels for 6% -> 6%
where the time goes in v4:
time: 94.9 us; the launch traced here: 94.3 us
  starting transfers between devices  60.5 us (64%)
  waiting for transfers between devices  22.4 us (24%)
  Pallas kernels  10.4 us (11%)
    ppermute x6, starting transfers between devices, swap_y(): return lax.ppermute(x, 'mp', [(i, i ^ 2 * pair) for i in range(n)])  19.3 us
    ppermute x3, starting transfers between devices, along_section(): return lax.ppermute(x, 'section', [(i, (i + by) % n) for i in range(n)])  15.4 us
    ppermute x1, starting transfers between devices, swap_core(): return lax.ppermute(x, 'mp', [(i, i ^ 1) for i in range(n)])  12.4 us
    all_to_all x1, waiting for transfers between devices, local(): lax.all_to_all(section_out, 'dp', split_axis=0, concat_axis=0, tiled=True)  7.24 us
    all_to_all x1, starting transfers between devices, local(): lax.all_to_all(partial_sums(got, scaled, lax.axis_size('mp')), 'mp', spli...  7.18 us
    all_to_all x1, starting transfers between devices, local(): lax.all_to_all(section_out, 'dp', split_axis=0, concat_axis=0, tiled=True)  6.33 us
    all_to_all x1, waiting for transfers between devices, local(): lax.all_to_all(partial_sums(got, scaled, lax.axis_size('mp')), 'mp', spli...  5.29 us
    ppermute x3, waiting for transfers between devices, along_section(): return lax.ppermute(x, 'section', [(i, (i + by) % n) for i in range(n)])  5.1 us
  transfers between devices with their start and end apart: 12, of which 6 were waited for; matrix products, arithmetic and copies ran while one was open for 0% of the time, Pallas kernels for 6%

profile of v4, /device:TPU:1, one launch (start us, length us, event | category | flops | bytes accessed | tf_op | source)
XLA Modules:
  0.0 94.3 jit_solution(4284812479736135393)
XLA Ops:
  0.6 3.2 %sent_products.1 = (bf16[4,8,192,128]{3,2,1,0:T(8,128)(2,1)S(1)}, bf16[1024,768]{1,0:T(8,128)(2,1)S(1)}) custom-call(s32[1]{0:T(128)} %bitcast.me_ref, bf16[8,192,768]{2,1,0:T(8,128)(2,1)} %bitcast.13, bf16[1024,768]{1,0:T(8,128)(2,1)} %bitcast.16), custom_call_target="tpu_custom_call" | custom-call | flops 1207959552 | bytes 5898240 | tf_op jit(solution)/shard_map/sent_products/pallas_call | solution.py:73
  3.8 12.4 %collective-permute-start = (bf16[4,8,192,128]{3,2,1,0:T(8,128)(2,1)S(1)}, bf16[4,8,192,128]{3,2,1,0:T(8,128)(2,1)S(1)}, u32[]{:S(2)}, u32[]{:S(2)}) collective-permute-start(bf16[4,8,192,128]{3,2,1,0:T(8,128)(2,1)S(1)} %get-tuple-element.19), channel_id=1, source_target_pairs={{0,8},{8,0},{16,24},{24,16},{32,40},{40,32},{48,56},{56,48},{1,9},... | collective-permute-start | bytes 4718600 | tf_op jit(solution)/shard_map/ppermute | solution.py:19
  16.3 1.8 %own_far_product.1 = (f32[8,192,128]{2,1,0:T(8,128)S(1)}, bf16[576,768]{1,0:T(8,128)(2,1)S(1)}) custom-call(s32[1]{0:T(128)} %bitcast.me_ref, bf16[8,192,768]{2,1,0:T(8,128)(2,1)} %bitcast.14, bf16[1024,768]{1,0:T(8,128)(2,1)S(1)} %get-tuple-element.17.c_ref), custom_call_target="tpu_custom_call" | custom-call | flops 603979776 | bytes 3735552 | tf_op jit(solution)/shard_map/own_far_product/pallas_call | solution.py:103
  18.1 0.0 copy-start
  18.1 1.1 %collective-permute-done.r_ref.other_ref = bf16[4,8,192,128]{3,2,1,0:T(8,128)(2,1)S(1)} collective-permute-done((bf16[4,8,192,128]{3,2,1,0:T(8,128)(2,1)S(1)}, bf16[4,8,192,128]{3,2,1,0:T(8,128)(2,1)S(1)}, u32[]{:S(2)}, u32[]{:S(2)}) %collective-permute-start) | collective-permute-done | bytes 1572896 | tf_op jit(solution)/shard_map/ppermute | solution.py:19
  19.3 0.1 far_sum.1
  19.4 1.9 %collective-permute-start.3 = (bf16[8,96,128]{2,1,0:T(8,128)(2,1)S(1)}, bf16[8,96,128]{2,1,0:T(8,128)(2,1)S(1)}, u32[]{:S(2)}, u32[]{:S(2)}) collective-permute-start(bf16[8,96,128]{2,1,0:T(8,128)(2,1)S(1)} %get-tuple-element.27), channel_id=1, source_target_pairs={{0,16},{8,24},{16,0},{24,8},{32,48},{40,56},{48,32},{56,40},{1,17}... | collective-permute-start | bytes 589832 | tf_op jit(solution)/shard_map/ppermute | solution.py:24
  21.3 1.9 %collective-permute-start.4 = (bf16[8,96,128]{2,1,0:T(8,128)(2,1)S(1)}, bf16[8,96,128]{2,1,0:T(8,128)(2,1)S(1)}, u32[]{:S(2)}, u32[]{:S(2)}) collective-permute-start(bf16[8,96,128]{2,1,0:T(8,128)(2,1)S(1)} %get-tuple-element.28), channel_id=1, source_target_pairs={{0,48},{8,56},{16,32},{24,40},{32,16},{40,24},{48,0},{56,8},{1,49}... | collective-permute-start | bytes 589832 | tf_op jit(solution)/shard_map/ppermute | solution.py:24
  23.2 0.0 copy-done
  23.2 0.0 copy-start.1
  23.2 0.0 copy-start.2
  23.2 1.1 %near_sum.1 = (bf16[8,96,128]{2,1,0:T(8,128)(2,1)S(1)}, bf16[8,96,128]{2,1,0:T(8,128)(2,1)S(1)}, f32[8,96,128]{2,1,0:T(8,128)S(1)}, f32[8,96,128]{2,1,0:T(8,128)S(1)}, f32[8,192,128]{2,1,0:T(8,128)S(1)}) custom-call(bf16[576,768]{1,0:T(8,128)(2,1)S(1)} %get-tuple-element.18.w_ref, bf16[1024,768]{1,0:T(8,128)(2,1)S(1)} %get-tuple-element.17.c_ref, ...), custom_call_target="tpu_custom_call" | custom-call | flops 905969664 | bytes 4816896 | tf_op jit(solution)/shard_map/near_sum/pallas_call | solution.py:147
  24.4 4.3 %collective-permute-start.1 = (bf16[8,96,128]{2,1,0:T(8,128)(2,1)S(1)}, bf16[8,96,128]{2,1,0:T(8,128)(2,1)S(1)}, u32[]{:S(2)}, u32[]{:S(2)}) collective-permute-start(bf16[8,96,128]{2,1,0:T(8,128)(2,1)S(1)} %get-tuple-element.21), channel_id=1, source_target_pairs={{0,16},{8,24},{16,0},{24,8},{32,48},{40,56},{48,32},{56,40},{1,17}... | collective-permute-start | bytes 589832 | tf_op jit(solution)/shard_map/ppermute | solution.py:24
  28.6 5.5 %collective-permute-start.2 = (bf16[8,96,128]{2,1,0:T(8,128)(2,1)S(1)}, bf16[8,96,128]{2,1,0:T(8,128)(2,1)S(1)}, u32[]{:S(2)}, u32[]{:S(2)}) collective-permute-start(bf16[8,96,128]{2,1,0:T(8,128)(2,1)S(1)} %get-tuple-element.22), channel_id=1, source_target_pairs={{0,48},{8,56},{16,32},{24,40},{32,16},{40,24},{48,0},{56,8},{1,49}... | collective-permute-start | bytes 589832 | tf_op jit(solution)/shard_map/ppermute | solution.py:24
  34.1 0.0 collective-permute-done.3.from_one_ref
  34.1 1.4 %collective-permute-done.4.from_three_ref = bf16[8,96,128]{2,1,0:T(8,128)(2,1)S(1)} collective-permute-done((bf16[8,96,128]{2,1,0:T(8,128)(2,1)S(1)}, bf16[8,96,128]{2,1,0:T(8,128)(2,1)S(1)}, u32[]{:S(2)}, u32[]{:S(2)}) %collective-permute-start.4) | collective-permute-done | bytes 196640 | tf_op jit(solution)/shard_map/ppermute | solution.py:24
  35.6 0.1 relay_sum.1
  35.6 1.9 %collective-permute-start.5 = (bf16[8,96,128]{2,1,0:T(8,128)(2,1)S(1)}, bf16[8,96,128]{2,1,0:T(8,128)(2,1)S(1)}, u32[]{:S(2)}, u32[]{:S(2)}) collective-permute-start(bf16[8,96,128]{2,1,0:T(8,128)(2,1)S(1)} %get-tuple-element.29), channel_id=1, source_target_pairs={{0,48},{8,56},{16,32},{24,40},{32,16},{40,24},{48,0},{56,8},{1,49}... | collective-permute-start | bytes 589832 | tf_op jit(solution)/shard_map/ppermute | solution.py:24
  37.6 3.8 %collective-permute-start.6 = (bf16[8,96,128]{2,1,0:T(8,128)(2,1)S(1)}, bf16[8,96,128]{2,1,0:T(8,128)(2,1)S(1)}, u32[]{:S(2)}, u32[]{:S(2)}) collective-permute-start(bf16[8,96,128]{2,1,0:T(8,128)(2,1)S(1)} %get-tuple-element.30), channel_id=1, source_target_pairs={{0,16},{8,24},{16,0},{24,8},{32,48},{40,56},{48,32},{56,40},{1,17}... | collective-permute-start | bytes 589832 | tf_op jit(solution)/shard_map/ppermute | solution.py:24
  41.3 0.0 collective-permute-done.1.top_ref
  41.4 2.2 %collective-permute-done.2.low_ref = bf16[8,96,128]{2,1,0:T(8,128)(2,1)S(1)} collective-permute-done((bf16[8,96,128]{2,1,0:T(8,128)(2,1)S(1)}, bf16[8,96,128]{2,1,0:T(8,128)(2,1)S(1)}, u32[]{:S(2)}, u32[]{:S(2)}) %collective-permute-start.2) | collective-permute-done | bytes 196640 | tf_op jit(solution)/shard_map/ppermute | solution.py:24
  43.5 0.0 copy-done.1
  43.5 0.0 copy-done.2
  43.5 0.1 add_direct.1
  43.7 11.5 %collective-permute-start.8 = (bf16[144,1536]{1,0:T(8,128)(2,1)S(1)}, bf16[144,1536]{1,0:T(8,128)(2,1)S(1)}, u32[]{:S(2)}, u32[]{:S(2)}) collective-permute-start(bf16[144,1536]{1,0:T(8,128)(2,1)S(1)} %get-tuple-element.31), channel_id=1, source_target_pairs={{0,704},{64,0},{128,64},{192,128},{256,192},{320,256},{384,320},{4... | collective-permute-start | bytes 1327112 | tf_op jit(solution)/shard_map/ppermute | solution.py:29
  55.2 0.0 collective-permute-done.5.top_ref
  55.2 0.0 collective-permute-done.6.low_ref
  55.2 0.8 add_last.1
  56.0 6.3 %all-to-all-start = ((bf16[8,192,128]{2,1,0:T(8,128)(2,1)}), bf16[8,192,128]{2,1,0:T(8,128)(2,1)S(1)}, u32[]{:S(2)}, u32[]{:S(2)}) async-start(bf16[8,192,128]{2,1,0:T(8,128)(2,1)} %add_last.1), calls=%async_computation | async-start | bytes 786432 | tf_op jit(solution)/shard_map/all_to_all | solution.py:293
  62.4 0.0 collective-permute-done.8.pack_ref
  62.4 0.3 scaled_cotangent.1.s_ref
  62.7 7.2 %all-to-all-done.x_ref = bf16[8,192,128]{2,1,0:T(8,128)(2,1)S(1)} async-done(((bf16[8,192,128]{2,1,0:T(8,128)(2,1)}), bf16[8,192,128]{2,1,0:T(8,128)(2,1)S(1)}, u32[]{:S(2)}, u32[]{:S(2)}) %all-to-all-start) | async-done | bytes 393248 | tf_op jit(solution)/shard_map/all_to_all | solution.py:293
  69.9 0.9 partial_sums.1
  70.8 7.2 %all-to-all-start.1 = ((f32[8,8,128]{2,1,0:T(8,128)}), f32[8,8,128]{2,1,0:T(8,128)S(1)}, u32[]{:S(2)}, u32[]{:S(2)}) async-start(f32[8,8,128]{2,1,0:T(8,128)} %partial_sums.1), calls=%async_computation.1 | async-start | bytes 65536 | tf_op jit(solution)/shard_map/all_to_all | solution.py:297
  78.0 1.9 %collective-permute-start.7 = (bf16[8,192,128]{2,1,0:T(8,128)(2,1)S(1)}, bf16[8,192,128]{2,1,0:T(8,128)(2,1)S(1)}, u32[]{:S(2)}, u32[]{:S(2)}) collective-permute-start(bf16[8,192,128]{2,1,0:T(8,128)(2,1)S(1)} %all-to-all-done.x_ref), channel_id=1, source_target_pairs={{0,64},{64,128},{128,192},{192,256},{256,320},{320,384},{384,448},... | collective-permute-start | bytes 1179656 | tf_op jit(solution)/shard_map/ppermute | solution.py:29
  79.9 5.3 %all-to-all-done.1.s_ref = f32[8,8,128]{2,1,0:T(8,128)S(1)} async-done(((f32[8,8,128]{2,1,0:T(8,128)}), f32[8,8,128]{2,1,0:T(8,128)S(1)}, u32[]{:S(2)}, u32[]{:S(2)}) %all-to-all-start.1) | async-done | bytes 32800 | tf_op jit(solution)/shard_map/all_to_all | solution.py:297
  85.2 0.0 copy-start.3
  85.2 1.9 %collective-permute-start.9 = (f32[8,128]{1,0:T(8,128)S(1)}, f32[8,128]{1,0:T(8,128)S(1)}, u32[]{:S(2)}, u32[]{:S(2)}) collective-permute-start(f32[8,128]{1,0:T(8,128)S(1)} %statistics.1.st_ref), channel_id=1, source_target_pairs={{0,64},{64,128},{128,192},{192,256},{256,320},{320,384},{384,448},... | collective-permute-start | bytes 12296 | tf_op jit(solution)/shard_map/ppermute | solution.py:29
  87.1 1.0 %gradient.1 = bf16[128,1536]{1,0:T(8,128)(2,1)} custom-call(bf16[8,192,128]{2,1,0:T(8,128)(2,1)S(1)} %all-to-all-done.x_ref, f32[1536,128]{1,0:T(8,128)S(1)} %scaled_cotangent.1.s_ref, f32[8,128]{1,0:T(8,128)S(1)} %statistics.1.st_ref), custom_call_target="tpu_custom_call" | custom-call | flops 11796480000 | bytes 1183744 | tf_op jit(solution)/shard_map/gradient/pallas_call | solution.py:206
  88.1 5.1 %collective-permute-done.9.st_ref = f32[8,128]{1,0:T(8,128)S(1)} collective-permute-done((f32[8,128]{1,0:T(8,128)S(1)}, f32[8,128]{1,0:T(8,128)S(1)}, u32[]{:S(2)}, u32[]{:S(2)}) %collective-permute-start.9) | collective-permute-done | bytes 4128 | tf_op jit(solution)/shard_map/ppermute | solution.py:29
  93.2 0.0 collective-permute-done.7.x_ref
  93.2 0.0 copy-done.3
  93.3 1.0 %layer_norm.1 = bf16[128,1536]{1,0:T(8,128)(2,1)} custom-call(bf16[8,192,128]{2,1,0:T(8,128)(2,1)S(1)} %collective-permute-done.7.x_ref, f32[8,128]{1,0:T(8,128)S(1)} %collective-permute-done.9.st_ref, f32[1,1536]{1,0:T(1,128)S(1)} %copy-done.2, f32[1,1536]{1,0:T(1,128)S(1)} %copy-done.3), custom_call_target="tpu_custom_call" | custom-call | flops 786432 | bytes 409600 | tf_op jit(solution)/shard_map/layer_norm/pallas_call | solution.py:206
  (3 shorter events, 0.0 us)
Async XLA Ops:
  3.8 15.4 %collective-permute-start = (bf16[4,8,192,128]{3,2,1,0:T(8,128)(2,1)S(1)}, bf16[4,8,192,128]{3,2,1,0:T(8,128)(2,1)S(1)}, u32[]{:S(2)}, u32[]{:S(2)}) collective-permute-start(bf16[4,8,192,128]{3,2,1,0:T(8,128)(2,1)S(1)} %get-tuple-element.19), channel_id=1, source_target_pairs={{0,8},{8,0},{16,24},{24,16},{32,40},{40,32},{48,56},{56,48},{1,9},... | collective-permute-start | bytes 4718600 | tf_op jit(solution)/shard_map/ppermute | solution.py:19
  18.1 5.1 %copy-start = (bf16[1,1024,192]{1,2,0:T(8,128)(2,1)S(1)}, bf16[1,1024,192]{1,2,0:T(8,128)(2,1)}, u32[]{:S(2)}) copy-start(bf16[1,1024,192]{1,2,0:T(8,128)(2,1)} %param.8) | copy-start | bytes 1179652
  19.4 14.8 %collective-permute-start.3 = (bf16[8,96,128]{2,1,0:T(8,128)(2,1)S(1)}, bf16[8,96,128]{2,1,0:T(8,128)(2,1)S(1)}, u32[]{:S(2)}, u32[]{:S(2)}) collective-permute-start(bf16[8,96,128]{2,1,0:T(8,128)(2,1)S(1)} %get-tuple-element.27), channel_id=1, source_target_pairs={{0,16},{8,24},{16,0},{24,8},{32,48},{40,56},{48,32},{56,40},{1,17}... | collective-permute-start | bytes 589832 | tf_op jit(solution)/shard_map/ppermute | solution.py:24
  21.3 14.3 %collective-permute-start.4 = (bf16[8,96,128]{2,1,0:T(8,128)(2,1)S(1)}, bf16[8,96,128]{2,1,0:T(8,128)(2,1)S(1)}, u32[]{:S(2)}, u32[]{:S(2)}) collective-permute-start(bf16[8,96,128]{2,1,0:T(8,128)(2,1)S(1)} %get-tuple-element.28), channel_id=1, source_target_pairs={{0,48},{8,56},{16,32},{24,40},{32,16},{40,24},{48,0},{56,8},{1,49}... | collective-permute-start | bytes 589832 | tf_op jit(solution)/shard_map/ppermute | solution.py:24
  23.2 20.3 %copy-start.1 = (bf16[1,128,1536]{2,1,0:T(8,128)(2,1)S(1)}, bf16[1,128,1536]{2,1,0:T(8,128)(2,1)}, u32[]{:S(2)}) copy-start(bf16[1,128,1536]{2,1,0:T(8,128)(2,1)} %param.11) | copy-start | bytes 1179652
  23.2 20.3 %copy-start.2 = (f32[1,1536]{1,0:T(1,128)S(1)}, f32[1,1536]{1,0:T(1,128)}, u32[]{:S(2)}) copy-start(f32[1,1536]{1,0:T(1,128)} %g_ref.1) | copy-start | bytes 18436
  24.4 17.0 %collective-permute-start.1 = (bf16[8,96,128]{2,1,0:T(8,128)(2,1)S(1)}, bf16[8,96,128]{2,1,0:T(8,128)(2,1)S(1)}, u32[]{:S(2)}, u32[]{:S(2)}) collective-permute-start(bf16[8,96,128]{2,1,0:T(8,128)(2,1)S(1)} %get-tuple-element.21), channel_id=1, source_target_pairs={{0,16},{8,24},{16,0},{24,8},{32,48},{40,56},{48,32},{56,40},{1,17}... | collective-permute-start | bytes 589832 | tf_op jit(solution)/shard_map/ppermute | solution.py:24
  28.6 14.9 %collective-permute-start.2 = (bf16[8,96,128]{2,1,0:T(8,128)(2,1)S(1)}, bf16[8,96,128]{2,1,0:T(8,128)(2,1)S(1)}, u32[]{:S(2)}, u32[]{:S(2)}) collective-permute-start(bf16[8,96,128]{2,1,0:T(8,128)(2,1)S(1)} %get-tuple-element.22), channel_id=1, source_target_pairs={{0,48},{8,56},{16,32},{24,40},{32,16},{40,24},{48,0},{56,8},{1,49}... | collective-permute-start | bytes 589832 | tf_op jit(solution)/shard_map/ppermute | solution.py:24
  35.6 19.5 %collective-permute-start.5 = (bf16[8,96,128]{2,1,0:T(8,128)(2,1)S(1)}, bf16[8,96,128]{2,1,0:T(8,128)(2,1)S(1)}, u32[]{:S(2)}, u32[]{:S(2)}) collective-permute-start(bf16[8,96,128]{2,1,0:T(8,128)(2,1)S(1)} %get-tuple-element.29), channel_id=1, source_target_pairs={{0,48},{8,56},{16,32},{24,40},{32,16},{40,24},{48,0},{56,8},{1,49}... | collective-permute-start | bytes 589832 | tf_op jit(solution)/shard_map/ppermute | solution.py:24
  37.6 17.6 %collective-permute-start.6 = (bf16[8,96,128]{2,1,0:T(8,128)(2,1)S(1)}, bf16[8,96,128]{2,1,0:T(8,128)(2,1)S(1)}, u32[]{:S(2)}, u32[]{:S(2)}) collective-permute-start(bf16[8,96,128]{2,1,0:T(8,128)(2,1)S(1)} %get-tuple-element.30), channel_id=1, source_target_pairs={{0,16},{8,24},{16,0},{24,8},{32,48},{40,56},{48,32},{56,40},{1,17}... | collective-permute-start | bytes 589832 | tf_op jit(solution)/shard_map/ppermute | solution.py:24
  43.7 18.7 %collective-permute-start.8 = (bf16[144,1536]{1,0:T(8,128)(2,1)S(1)}, bf16[144,1536]{1,0:T(8,128)(2,1)S(1)}, u32[]{:S(2)}, u32[]{:S(2)}) collective-permute-start(bf16[144,1536]{1,0:T(8,128)(2,1)S(1)} %get-tuple-element.31), channel_id=1, source_target_pairs={{0,704},{64,0},{128,64},{192,128},{256,192},{320,256},{384,320},{4... | collective-permute-start | bytes 1327112 | tf_op jit(solution)/shard_map/ppermute | solution.py:29
  56.0 13.9 %all-to-all-start = ((bf16[8,192,128]{2,1,0:T(8,128)(2,1)}), bf16[8,192,128]{2,1,0:T(8,128)(2,1)S(1)}, u32[]{:S(2)}, u32[]{:S(2)}) async-start(bf16[8,192,128]{2,1,0:T(8,128)(2,1)} %add_last.1), calls=%async_computation | async-start | bytes 786432 | tf_op jit(solution)/shard_map/all_to_all | solution.py:293
  70.8 14.4 %all-to-all-start.1 = ((f32[8,8,128]{2,1,0:T(8,128)}), f32[8,8,128]{2,1,0:T(8,128)S(1)}, u32[]{:S(2)}, u32[]{:S(2)}) async-start(f32[8,8,128]{2,1,0:T(8,128)} %partial_sums.1), calls=%async_computation.1 | async-start | bytes 65536 | tf_op jit(solution)/shard_map/all_to_all | solution.py:297
  78.0 15.3 %collective-permute-start.7 = (bf16[8,192,128]{2,1,0:T(8,128)(2,1)S(1)}, bf16[8,192,128]{2,1,0:T(8,128)(2,1)S(1)}, u32[]{:S(2)}, u32[]{:S(2)}) collective-permute-start(bf16[8,192,128]{2,1,0:T(8,128)(2,1)S(1)} %all-to-all-done.x_ref), channel_id=1, source_target_pairs={{0,64},{64,128},{128,192},{192,256},{256,320},{320,384},{384,448},... | collective-permute-start | bytes 1179656 | tf_op jit(solution)/shard_map/ppermute | solution.py:29
  85.2 8.1 %copy-start.3 = (f32[1,1536]{1,0:T(1,128)S(1)}, f32[1,1536]{1,0:T(1,128)}, u32[]{:S(2)}) copy-start(f32[1,1536]{1,0:T(1,128)} %b_ref.1) | copy-start | bytes 18436
  85.2 8.0 %collective-permute-start.9 = (f32[8,128]{1,0:T(8,128)S(1)}, f32[8,128]{1,0:T(8,128)S(1)}, u32[]{:S(2)}, u32[]{:S(2)}) collective-permute-start(f32[8,128]{1,0:T(8,128)S(1)} %statistics.1.st_ref), channel_id=1, source_target_pairs={{0,64},{64,128},{128,192},{192,256},{256,320},{320,384},{384,448},... | collective-permute-start | bytes 12296 | tf_op jit(solution)/shard_map/ppermute | solution.py:29

commit v5 on v4

--- a/solution.py
+++ b/solution.py
@@ -221,12 +221,16 @@
 def partial_sums(x, scaled, copies):
     def body(x_ref, s_ref, o_ref):
         groups, rows = x.shape[:2]
-        totals = [jnp.zeros((rows, TB), F32)] * 4
-        for i in range(groups):
-            v = x_ref[i].astype(F32)
-            s = s_ref[i * rows:(i + 1) * rows]
-            totals = [t + a for t, a in zip(totals, (v, v * v, s, s * v))]
-        sums = [jnp.sum(t, axis=0, keepdims=True) for t in totals]
+        part = 48
+        sums = [jnp.zeros((8, TB), F32)] * 4
+        for r in range(0, rows, part):
+            totals = [jnp.zeros((part, TB), F32)] * 4
+            for i in range(groups):
+                v = x_ref[i, r:r + part].astype(F32)
+                s = s_ref[i * rows + r:i * rows + r + part]
+                totals = [t + a for t, a in zip(totals, (v, v * v, s, s * v))]
+            sums = [a + jnp.sum(t.reshape(part // 8, 8, TB), axis=0) for a, t in zip(sums, totals)]
+        sums = [jnp.sum(a, axis=0, keepdims=True) for a in sums]
         block = jnp.concatenate([*sums, jnp.zeros((4, TB), F32)], axis=0)
         for i in range(copies):
             o_ref[i] = block

time: 94.9 us -> 94.8 us (level)
  no operation moved by 1% of the time
where the time goes in v5:
time: 94.8 us; the launch traced here: 94.2 us
  starting transfers between devices  60.5 us (64%)
  waiting for transfers between devices  22.4 us (24%)
  Pallas kernels  10.3 us (11%)
    ppermute x6, starting transfers between devices, swap_y(): return lax.ppermute(x, 'mp', [(i, i ^ 2 * pair) for i in range(n)])  19.3 us
    ppermute x3, starting transfers between devices, along_section(): return lax.ppermute(x, 'section', [(i, (i + by) % n) for i in range(n)])  15.4 us
    ppermute x1, starting transfers between devices, swap_core(): return lax.ppermute(x, 'mp', [(i, i ^ 1) for i in range(n)])  12.4 us
    all_to_all x1, waiting for transfers between devices, local(): lax.all_to_all(section_out, 'dp', split_axis=0, concat_axis=0, tiled=True)  7.24 us
    all_to_all x1, starting transfers between devices, local(): lax.all_to_all(partial_sums(got, scaled, lax.axis_size('mp')), 'mp', spli...  7.18 us
    all_to_all x1, starting transfers between devices, local(): lax.all_to_all(section_out, 'dp', split_axis=0, concat_axis=0, tiled=True)  6.33 us
    all_to_all x1, waiting for transfers between devices, local(): lax.all_to_all(partial_sums(got, scaled, lax.axis_size('mp')), 'mp', spli...  5.29 us
    ppermute x3, waiting for transfers between devices, along_section(): return lax.ppermute(x, 'section', [(i, (i + by) % n) for i in range(n)])  5.1 us
  transfers between devices with their start and end apart: 12, of which 6 were waited for; matrix products, arithmetic and copies ran while one was open for 0% of the time, Pallas kernels for 6%

profile of v5, /device:TPU:1, one launch (start us, length us, event | category | flops | bytes accessed | tf_op | source)
XLA Modules:
  0.0 94.2 jit_solution(13637682388252108847)
XLA Ops:
  0.6 3.2 %sent_products.1 = (bf16[4,8,192,128]{3,2,1,0:T(8,128)(2,1)S(1)}, bf16[1024,768]{1,0:T(8,128)(2,1)S(1)}) custom-call(s32[1]{0:T(128)} %bitcast.me_ref, bf16[8,192,768]{2,1,0:T(8,128)(2,1)} %bitcast.13, bf16[1024,768]{1,0:T(8,128)(2,1)} %bitcast.16), custom_call_target="tpu_custom_call" | custom-call | flops 1207959552 | bytes 5898240 | tf_op jit(solution)/shard_map/sent_products/pallas_call | solution.py:73
  3.8 12.4 %collective-permute-start = (bf16[4,8,192,128]{3,2,1,0:T(8,128)(2,1)S(1)}, bf16[4,8,192,128]{3,2,1,0:T(8,128)(2,1)S(1)}, u32[]{:S(2)}, u32[]{:S(2)}) collective-permute-start(bf16[4,8,192,128]{3,2,1,0:T(8,128)(2,1)S(1)} %get-tuple-element.19), channel_id=1, source_target_pairs={{0,8},{8,0},{16,24},{24,16},{32,40},{40,32},{48,56},{56,48},{1,9},... | collective-permute-start | bytes 4718600 | tf_op jit(solution)/shard_map/ppermute | solution.py:19
  16.3 1.8 %own_far_product.1 = (f32[8,192,128]{2,1,0:T(8,128)S(1)}, bf16[576,768]{1,0:T(8,128)(2,1)S(1)}) custom-call(s32[1]{0:T(128)} %bitcast.me_ref, bf16[8,192,768]{2,1,0:T(8,128)(2,1)} %bitcast.14, bf16[1024,768]{1,0:T(8,128)(2,1)S(1)} %get-tuple-element.17.c_ref), custom_call_target="tpu_custom_call" | custom-call | flops 603979776 | bytes 3735552 | tf_op jit(solution)/shard_map/own_far_product/pallas_call | solution.py:103
  18.1 0.0 copy-start
  18.1 1.1 %collective-permute-done.r_ref.other_ref = bf16[4,8,192,128]{3,2,1,0:T(8,128)(2,1)S(1)} collective-permute-done((bf16[4,8,192,128]{3,2,1,0:T(8,128)(2,1)S(1)}, bf16[4,8,192,128]{3,2,1,0:T(8,128)(2,1)S(1)}, u32[]{:S(2)}, u32[]{:S(2)}) %collective-permute-start) | collective-permute-done | bytes 1572896 | tf_op jit(solution)/shard_map/ppermute | solution.py:19
  19.3 0.1 far_sum.1
  19.4 1.9 %collective-permute-start.3 = (bf16[8,96,128]{2,1,0:T(8,128)(2,1)S(1)}, bf16[8,96,128]{2,1,0:T(8,128)(2,1)S(1)}, u32[]{:S(2)}, u32[]{:S(2)}) collective-permute-start(bf16[8,96,128]{2,1,0:T(8,128)(2,1)S(1)} %get-tuple-element.27), channel_id=1, source_target_pairs={{0,16},{8,24},{16,0},{24,8},{32,48},{40,56},{48,32},{56,40},{1,17}... | collective-permute-start | bytes 589832 | tf_op jit(solution)/shard_map/ppermute | solution.py:24
  21.3 1.9 %collective-permute-start.4 = (bf16[8,96,128]{2,1,0:T(8,128)(2,1)S(1)}, bf16[8,96,128]{2,1,0:T(8,128)(2,1)S(1)}, u32[]{:S(2)}, u32[]{:S(2)}) collective-permute-start(bf16[8,96,128]{2,1,0:T(8,128)(2,1)S(1)} %get-tuple-element.28), channel_id=1, source_target_pairs={{0,48},{8,56},{16,32},{24,40},{32,16},{40,24},{48,0},{56,8},{1,49}... | collective-permute-start | bytes 589832 | tf_op jit(solution)/shard_map/ppermute | solution.py:24
  23.2 0.0 copy-done
  23.2 0.0 copy-start.1
  23.2 0.0 copy-start.2
  23.2 1.1 %near_sum.1 = (bf16[8,96,128]{2,1,0:T(8,128)(2,1)S(1)}, bf16[8,96,128]{2,1,0:T(8,128)(2,1)S(1)}, f32[8,96,128]{2,1,0:T(8,128)S(1)}, f32[8,96,128]{2,1,0:T(8,128)S(1)}, f32[8,192,128]{2,1,0:T(8,128)S(1)}) custom-call(bf16[576,768]{1,0:T(8,128)(2,1)S(1)} %get-tuple-element.18.w_ref, bf16[1024,768]{1,0:T(8,128)(2,1)S(1)} %get-tuple-element.17.c_ref, ...), custom_call_target="tpu_custom_call" | custom-call | flops 905969664 | bytes 4816896 | tf_op jit(solution)/shard_map/near_sum/pallas_call | solution.py:147
  24.4 4.3 %collective-permute-start.1 = (bf16[8,96,128]{2,1,0:T(8,128)(2,1)S(1)}, bf16[8,96,128]{2,1,0:T(8,128)(2,1)S(1)}, u32[]{:S(2)}, u32[]{:S(2)}) collective-permute-start(bf16[8,96,128]{2,1,0:T(8,128)(2,1)S(1)} %get-tuple-element.21), channel_id=1, source_target_pairs={{0,16},{8,24},{16,0},{24,8},{32,48},{40,56},{48,32},{56,40},{1,17}... | collective-permute-start | bytes 589832 | tf_op jit(solution)/shard_map/ppermute | solution.py:24
  28.6 5.5 %collective-permute-start.2 = (bf16[8,96,128]{2,1,0:T(8,128)(2,1)S(1)}, bf16[8,96,128]{2,1,0:T(8,128)(2,1)S(1)}, u32[]{:S(2)}, u32[]{:S(2)}) collective-permute-start(bf16[8,96,128]{2,1,0:T(8,128)(2,1)S(1)} %get-tuple-element.22), channel_id=1, source_target_pairs={{0,48},{8,56},{16,32},{24,40},{32,16},{40,24},{48,0},{56,8},{1,49}... | collective-permute-start | bytes 589832 | tf_op jit(solution)/shard_map/ppermute | solution.py:24
  34.1 0.0 collective-permute-done.3.from_one_ref
  34.1 1.4 %collective-permute-done.4.from_three_ref = bf16[8,96,128]{2,1,0:T(8,128)(2,1)S(1)} collective-permute-done((bf16[8,96,128]{2,1,0:T(8,128)(2,1)S(1)}, bf16[8,96,128]{2,1,0:T(8,128)(2,1)S(1)}, u32[]{:S(2)}, u32[]{:S(2)}) %collective-permute-start.4) | collective-permute-done | bytes 196640 | tf_op jit(solution)/shard_map/ppermute | solution.py:24
  35.6 0.1 relay_sum.1
  35.6 1.9 %collective-permute-start.5 = (bf16[8,96,128]{2,1,0:T(8,128)(2,1)S(1)}, bf16[8,96,128]{2,1,0:T(8,128)(2,1)S(1)}, u32[]{:S(2)}, u32[]{:S(2)}) collective-permute-start(bf16[8,96,128]{2,1,0:T(8,128)(2,1)S(1)} %get-tuple-element.29), channel_id=1, source_target_pairs={{0,48},{8,56},{16,32},{24,40},{32,16},{40,24},{48,0},{56,8},{1,49}... | collective-permute-start | bytes 589832 | tf_op jit(solution)/shard_map/ppermute | solution.py:24
  37.6 3.8 %collective-permute-start.6 = (bf16[8,96,128]{2,1,0:T(8,128)(2,1)S(1)}, bf16[8,96,128]{2,1,0:T(8,128)(2,1)S(1)}, u32[]{:S(2)}, u32[]{:S(2)}) collective-permute-start(bf16[8,96,128]{2,1,0:T(8,128)(2,1)S(1)} %get-tuple-element.30), channel_id=1, source_target_pairs={{0,16},{8,24},{16,0},{24,8},{32,48},{40,56},{48,32},{56,40},{1,17}... | collective-permute-start | bytes 589832 | tf_op jit(solution)/shard_map/ppermute | solution.py:24
  41.3 0.0 collective-permute-done.1.top_ref
  41.4 2.2 %collective-permute-done.2.low_ref = bf16[8,96,128]{2,1,0:T(8,128)(2,1)S(1)} collective-permute-done((bf16[8,96,128]{2,1,0:T(8,128)(2,1)S(1)}, bf16[8,96,128]{2,1,0:T(8,128)(2,1)S(1)}, u32[]{:S(2)}, u32[]{:S(2)}) %collective-permute-start.2) | collective-permute-done | bytes 196640 | tf_op jit(solution)/shard_map/ppermute | solution.py:24
  43.5 0.0 copy-done.1
  43.5 0.0 copy-done.2
  43.5 0.1 add_direct.1
  43.7 11.5 %collective-permute-start.8 = (bf16[144,1536]{1,0:T(8,128)(2,1)S(1)}, bf16[144,1536]{1,0:T(8,128)(2,1)S(1)}, u32[]{:S(2)}, u32[]{:S(2)}) collective-permute-start(bf16[144,1536]{1,0:T(8,128)(2,1)S(1)} %get-tuple-element.31), channel_id=1, source_target_pairs={{0,704},{64,0},{128,64},{192,128},{256,192},{320,256},{384,320},{4... | collective-permute-start | bytes 1327112 | tf_op jit(solution)/shard_map/ppermute | solution.py:29
  55.2 0.0 collective-permute-done.5.top_ref
  55.2 0.0 collective-permute-done.6.low_ref
  55.2 0.8 add_last.1
  56.0 6.3 %all-to-all-start = ((bf16[8,192,128]{2,1,0:T(8,128)(2,1)}), bf16[8,192,128]{2,1,0:T(8,128)(2,1)S(1)}, u32[]{:S(2)}, u32[]{:S(2)}) async-start(bf16[8,192,128]{2,1,0:T(8,128)(2,1)} %add_last.1), calls=%async_computation | async-start | bytes 786432 | tf_op jit(solution)/shard_map/all_to_all | solution.py:297
  62.4 0.0 collective-permute-done.8.pack_ref
  62.4 0.3 scaled_cotangent.1.s_ref
  62.7 7.2 %all-to-all-done.x_ref = bf16[8,192,128]{2,1,0:T(8,128)(2,1)S(1)} async-done(((bf16[8,192,128]{2,1,0:T(8,128)(2,1)}), bf16[8,192,128]{2,1,0:T(8,128)(2,1)S(1)}, u32[]{:S(2)}, u32[]{:S(2)}) %all-to-all-start) | async-done | bytes 393248 | tf_op jit(solution)/shard_map/all_to_all | solution.py:297
  69.9 0.8 partial_sums.1
  70.7 7.2 %all-to-all-start.1 = ((f32[8,8,128]{2,1,0:T(8,128)}), f32[8,8,128]{2,1,0:T(8,128)S(1)}, u32[]{:S(2)}, u32[]{:S(2)}) async-start(f32[8,8,128]{2,1,0:T(8,128)} %partial_sums.1), calls=%async_computation.1 | async-start | bytes 65536 | tf_op jit(solution)/shard_map/all_to_all | solution.py:301
  77.9 1.9 %collective-permute-start.7 = (bf16[8,192,128]{2,1,0:T(8,128)(2,1)S(1)}, bf16[8,192,128]{2,1,0:T(8,128)(2,1)S(1)}, u32[]{:S(2)}, u32[]{:S(2)}) collective-permute-start(bf16[8,192,128]{2,1,0:T(8,128)(2,1)S(1)} %all-to-all-done.x_ref), channel_id=1, source_target_pairs={{0,64},{64,128},{128,192},{192,256},{256,320},{320,384},{384,448},... | collective-permute-start | bytes 1179656 | tf_op jit(solution)/shard_map/ppermute | solution.py:29
  79.8 5.3 %all-to-all-done.1.s_ref = f32[8,8,128]{2,1,0:T(8,128)S(1)} async-done(((f32[8,8,128]{2,1,0:T(8,128)}), f32[8,8,128]{2,1,0:T(8,128)S(1)}, u32[]{:S(2)}, u32[]{:S(2)}) %all-to-all-start.1) | async-done | bytes 32800 | tf_op jit(solution)/shard_map/all_to_all | solution.py:301
  85.1 0.0 copy-start.3
  85.1 1.9 %collective-permute-start.9 = (f32[8,128]{1,0:T(8,128)S(1)}, f32[8,128]{1,0:T(8,128)S(1)}, u32[]{:S(2)}, u32[]{:S(2)}) collective-permute-start(f32[8,128]{1,0:T(8,128)S(1)} %statistics.1.st_ref), channel_id=1, source_target_pairs={{0,64},{64,128},{128,192},{192,256},{256,320},{320,384},{384,448},... | collective-permute-start | bytes 12296 | tf_op jit(solution)/shard_map/ppermute | solution.py:29
  87.0 1.0 %gradient.1 = bf16[128,1536]{1,0:T(8,128)(2,1)} custom-call(bf16[8,192,128]{2,1,0:T(8,128)(2,1)S(1)} %all-to-all-done.x_ref, f32[1536,128]{1,0:T(8,128)S(1)} %scaled_cotangent.1.s_ref, f32[8,128]{1,0:T(8,128)S(1)} %statistics.1.st_ref), custom_call_target="tpu_custom_call" | custom-call | flops 11796480000 | bytes 1183744 | tf_op jit(solution)/shard_map/gradient/pallas_call | solution.py:206
  88.1 5.1 %collective-permute-done.9.st_ref = f32[8,128]{1,0:T(8,128)S(1)} collective-permute-done((f32[8,128]{1,0:T(8,128)S(1)}, f32[8,128]{1,0:T(8,128)S(1)}, u32[]{:S(2)}, u32[]{:S(2)}) %collective-permute-start.9) | collective-permute-done | bytes 4128 | tf_op jit(solution)/shard_map/ppermute | solution.py:29
  93.2 0.0 collective-permute-done.7.x_ref
  93.2 0.0 copy-done.3
  93.2 1.0 %layer_norm.1 = bf16[128,1536]{1,0:T(8,128)(2,1)} custom-call(bf16[8,192,128]{2,1,0:T(8,128)(2,1)S(1)} %collective-permute-done.7.x_ref, f32[8,128]{1,0:T(8,128)S(1)} %collective-permute-done.9.st_ref, f32[1,1536]{1,0:T(1,128)S(1)} %copy-done.2, f32[1,1536]{1,0:T(1,128)S(1)} %copy-done.3), custom_call_target="tpu_custom_call" | custom-call | flops 786432 | bytes 409600 | tf_op jit(solution)/shard_map/layer_norm/pallas_call | solution.py:206
  (3 shorter events, 0.0 us)
Async XLA Ops:
  3.8 15.4 %collective-permute-start = (bf16[4,8,192,128]{3,2,1,0:T(8,128)(2,1)S(1)}, bf16[4,8,192,128]{3,2,1,0:T(8,128)(2,1)S(1)}, u32[]{:S(2)}, u32[]{:S(2)}) collective-permute-start(bf16[4,8,192,128]{3,2,1,0:T(8,128)(2,1)S(1)} %get-tuple-element.19), channel_id=1, source_target_pairs={{0,8},{8,0},{16,24},{24,16},{32,40},{40,32},{48,56},{56,48},{1,9},... | collective-permute-start | bytes 4718600 | tf_op jit(solution)/shard_map/ppermute | solution.py:19
  18.1 5.1 %copy-start = (bf16[1,1024,192]{1,2,0:T(8,128)(2,1)S(1)}, bf16[1,1024,192]{1,2,0:T(8,128)(2,1)}, u32[]{:S(2)}) copy-start(bf16[1,1024,192]{1,2,0:T(8,128)(2,1)} %param.8) | copy-start | bytes 1179652
  19.4 14.8 %collective-permute-start.3 = (bf16[8,96,128]{2,1,0:T(8,128)(2,1)S(1)}, bf16[8,96,128]{2,1,0:T(8,128)(2,1)S(1)}, u32[]{:S(2)}, u32[]{:S(2)}) collective-permute-start(bf16[8,96,128]{2,1,0:T(8,128)(2,1)S(1)} %get-tuple-element.27), channel_id=1, source_target_pairs={{0,16},{8,24},{16,0},{24,8},{32,48},{40,56},{48,32},{56,40},{1,17}... | collective-permute-start | bytes 589832 | tf_op jit(solution)/shard_map/ppermute | solution.py:24
  21.3 14.3 %collective-permute-start.4 = (bf16[8,96,128]{2,1,0:T(8,128)(2,1)S(1)}, bf16[8,96,128]{2,1,0:T(8,128)(2,1)S(1)}, u32[]{:S(2)}, u32[]{:S(2)}) collective-permute-start(bf16[8,96,128]{2,1,0:T(8,128)(2,1)S(1)} %get-tuple-element.28), channel_id=1, source_target_pairs={{0,48},{8,56},{16,32},{24,40},{32,16},{40,24},{48,0},{56,8},{1,49}... | collective-permute-start | bytes 589832 | tf_op jit(solution)/shard_map/ppermute | solution.py:24
  23.2 20.3 %copy-start.1 = (bf16[1,128,1536]{2,1,0:T(8,128)(2,1)S(1)}, bf16[1,128,1536]{2,1,0:T(8,128)(2,1)}, u32[]{:S(2)}) copy-start(bf16[1,128,1536]{2,1,0:T(8,128)(2,1)} %param.11) | copy-start | bytes 1179652
  23.2 20.3 %copy-start.2 = (f32[1,1536]{1,0:T(1,128)S(1)}, f32[1,1536]{1,0:T(1,128)}, u32[]{:S(2)}) copy-start(f32[1,1536]{1,0:T(1,128)} %g_ref.1) | copy-start | bytes 18436
  24.4 17.0 %collective-permute-start.1 = (bf16[8,96,128]{2,1,0:T(8,128)(2,1)S(1)}, bf16[8,96,128]{2,1,0:T(8,128)(2,1)S(1)}, u32[]{:S(2)}, u32[]{:S(2)}) collective-permute-start(bf16[8,96,128]{2,1,0:T(8,128)(2,1)S(1)} %get-tuple-element.21), channel_id=1, source_target_pairs={{0,16},{8,24},{16,0},{24,8},{32,48},{40,56},{48,32},{56,40},{1,17}... | collective-permute-start | bytes 589832 | tf_op jit(solution)/shard_map/ppermute | solution.py:24
  28.6 14.9 %collective-permute-start.2 = (bf16[8,96,128]{2,1,0:T(8,128)(2,1)S(1)}, bf16[8,96,128]{2,1,0:T(8,128)(2,1)S(1)}, u32[]{:S(2)}, u32[]{:S(2)}) collective-permute-start(bf16[8,96,128]{2,1,0:T(8,128)(2,1)S(1)} %get-tuple-element.22), channel_id=1, source_target_pairs={{0,48},{8,56},{16,32},{24,40},{32,16},{40,24},{48,0},{56,8},{1,49}... | collective-permute-start | bytes 589832 | tf_op jit(solution)/shard_map/ppermute | solution.py:24
  35.6 19.5 %collective-permute-start.5 = (bf16[8,96,128]{2,1,0:T(8,128)(2,1)S(1)}, bf16[8,96,128]{2,1,0:T(8,128)(2,1)S(1)}, u32[]{:S(2)}, u32[]{:S(2)}) collective-permute-start(bf16[8,96,128]{2,1,0:T(8,128)(2,1)S(1)} %get-tuple-element.29), channel_id=1, source_target_pairs={{0,48},{8,56},{16,32},{24,40},{32,16},{40,24},{48,0},{56,8},{1,49}... | collective-permute-start | bytes 589832 | tf_op jit(solution)/shard_map/ppermute | solution.py:24
  37.6 17.6 %collective-permute-start.6 = (bf16[8,96,128]{2,1,0:T(8,128)(2,1)S(1)}, bf16[8,96,128]{2,1,0:T(8,128)(2,1)S(1)}, u32[]{:S(2)}, u32[]{:S(2)}) collective-permute-start(bf16[8,96,128]{2,1,0:T(8,128)(2,1)S(1)} %get-tuple-element.30), channel_id=1, source_target_pairs={{0,16},{8,24},{16,0},{24,8},{32,48},{40,56},{48,32},{56,40},{1,17}... | collective-permute-start | bytes 589832 | tf_op jit(solution)/shard_map/ppermute | solution.py:24
  43.7 18.7 %collective-permute-start.8 = (bf16[144,1536]{1,0:T(8,128)(2,1)S(1)}, bf16[144,1536]{1,0:T(8,128)(2,1)S(1)}, u32[]{:S(2)}, u32[]{:S(2)}) collective-permute-start(bf16[144,1536]{1,0:T(8,128)(2,1)S(1)} %get-tuple-element.31), channel_id=1, source_target_pairs={{0,704},{64,0},{128,64},{192,128},{256,192},{320,256},{384,320},{4... | collective-permute-start | bytes 1327112 | tf_op jit(solution)/shard_map/ppermute | solution.py:29
  56.0 13.9 %all-to-all-start = ((bf16[8,192,128]{2,1,0:T(8,128)(2,1)}), bf16[8,192,128]{2,1,0:T(8,128)(2,1)S(1)}, u32[]{:S(2)}, u32[]{:S(2)}) async-start(bf16[8,192,128]{2,1,0:T(8,128)(2,1)} %add_last.1), calls=%async_computation | async-start | bytes 786432 | tf_op jit(solution)/shard_map/all_to_all | solution.py:297
  70.7 14.4 %all-to-all-start.1 = ((f32[8,8,128]{2,1,0:T(8,128)}), f32[8,8,128]{2,1,0:T(8,128)S(1)}, u32[]{:S(2)}, u32[]{:S(2)}) async-start(f32[8,8,128]{2,1,0:T(8,128)} %partial_sums.1), calls=%async_computation.1 | async-start | bytes 65536 | tf_op jit(solution)/shard_map/all_to_all | solution.py:301
  77.9 15.3 %collective-permute-start.7 = (bf16[8,192,128]{2,1,0:T(8,128)(2,1)S(1)}, bf16[8,192,128]{2,1,0:T(8,128)(2,1)S(1)}, u32[]{:S(2)}, u32[]{:S(2)}) collective-permute-start(bf16[8,192,128]{2,1,0:T(8,128)(2,1)S(1)} %all-to-all-done.x_ref), channel_id=1, source_target_pairs={{0,64},{64,128},{128,192},{192,256},{256,320},{320,384},{384,448},... | collective-permute-start | bytes 1179656 | tf_op jit(solution)/shard_map/ppermute | solution.py:29
  85.1 8.1 %copy-start.3 = (f32[1,1536]{1,0:T(1,128)S(1)}, f32[1,1536]{1,0:T(1,128)}, u32[]{:S(2)}) copy-start(f32[1,1536]{1,0:T(1,128)} %b_ref.1) | copy-start | bytes 18436
  85.1 8.0 %collective-permute-start.9 = (f32[8,128]{1,0:T(8,128)S(1)}, f32[8,128]{1,0:T(8,128)S(1)}, u32[]{:S(2)}, u32[]{:S(2)}) collective-permute-start(f32[8,128]{1,0:T(8,128)S(1)} %statistics.1.st_ref), channel_id=1, source_target_pairs={{0,64},{64,128},{128,192},{192,256},{256,320},{320,384},{384,448},... | collective-permute-start | bytes 12296 | tf_op jit(solution)/shard_map/ppermute | solution.py:29
